TPU v7x, 32 devices: a whole 2x2x4 slice. The times are simulated.
32 devices in a mesh: sec: 4 (over y, core), cp: 8 (over z, x).
Axes of the slice: x: 2, y: 2, z: 4, core: 2. Of those that a mesh axis runs over, the one named last changes fastest.
Arguments:
- projected: bfloat16 [4096, 10240], P(('sec', 'cp')), may hold values from -6 to 6
- conv_weight: float32 [4, 10240], replicated, may hold values from -3 to 3
- conv_bias: float32 [10240], replicated, may hold values from -3 to 3
- step_size: bfloat16 [4096, 128], P(('sec', 'cp')), may hold values from 0 to 1
- log_decay: bfloat16 [4096, 128], P(('sec', 'cp')), may hold values from -1 to 0
- skip_gain: float32 [128], replicated, may hold values from 0.5 to 1.5
Outputs:
- ssd_out: bfloat16 [4096, 8192], P(('sec', 'cp'))
All inputs are finite; a program needn't handle non-finite values.
Results may differ from a plain program's by a relative error of at most 0.0034.
Values may be sent and summed in bfloat16 or wider, within the bound.
A program may use at most 64 MiB of HBM per device.

v0:
```python
import jax
import jax.numpy as jnp
from jax import lax
from jax.sharding import PartitionSpec as P

HEAD_COUNT = 128
P_SIZE = 64
N = 128
G = 8
BLOCK = 256
KERNEL = 4


def passed_along(value, axis, steps):
    count = lax.axis_size(axis)
    leading, last = (max(0, -steps), min(count, count - steps))
    return lax.ppermute(value, axis, [(source, source + steps) for source in range(leading, last)])


def causal_conv(columns, rim_rows, weights, biases):
    padded = jnp.concatenate([rim_rows, columns], 0)
    length = columns.shape[0]
    summed = biases[None, :] + weights[0][None, :] * padded[0:length].astype(jnp.float32)
    for offset in range(1, KERNEL):
        summed = summed + weights[offset][None, :] * padded[offset : offset + length].astype(
            jnp.float32
        )
    return jax.nn.silu(summed).astype(jnp.bfloat16)


def per_target(columns, row_count, targets, heads_here, group_heads):
    if heads_here >= group_heads:
        return columns.reshape(row_count, targets, heads_here // group_heads * N)
    return jnp.repeat(columns.reshape(row_count, G, N), group_heads // heads_here, axis=1)


def per_device(projected, conv_weight, conv_bias, step_size, log_decay, skip_gain):
    targets = lax.axis_size("cp")
    row_count = projected.shape[0]
    heads_here = HEAD_COUNT // targets
    group_heads = HEAD_COUNT // G
    groups_here = max(1, heads_here // group_heads)
    width_x = HEAD_COUNT * P_SIZE
    width_g = G * N
    rim_rows = passed_along(projected[row_count - (KERNEL - 1) :], ("sec", "cp"), 1)
    mixed_cols = causal_conv(projected, rim_rows, conv_weight, conv_bias)
    send_b = per_target(
        mixed_cols[:, width_x : width_x + width_g], row_count, targets, heads_here, group_heads
    )
    send_c = per_target(
        mixed_cols[:, width_x + width_g :], row_count, targets, heads_here, group_heads
    )
    send_bc = jnp.concatenate([send_b, send_c], axis=2).reshape(
        row_count, targets * 2 * groups_here * N
    )
    head_x, head_bc, head_step, head_decay = (
        lax.all_to_all(mixed_cols[:, :width_x], "cp", split_axis=1, concat_axis=0, tiled=True),
        lax.all_to_all(send_bc, "cp", split_axis=1, concat_axis=0, tiled=True),
        lax.all_to_all(step_size, "cp", split_axis=1, concat_axis=0, tiled=True),
        lax.all_to_all(log_decay, "cp", split_axis=1, concat_axis=0, tiled=True),
    )
    position = lax.axis_index("cp")
    section_rows = head_x.shape[0]
    blocks = section_rows // BLOCK
    repeat_count = heads_here // groups_here
    values = head_x.reshape(blocks, BLOCK, heads_here, P_SIZE)
    keys_b = jnp.repeat(
        head_bc[:, : groups_here * N].reshape(blocks, BLOCK, groups_here, N), repeat_count, axis=2
    )
    query_c = jnp.repeat(
        head_bc[:, groups_here * N :].reshape(blocks, BLOCK, groups_here, N), repeat_count, axis=2
    )
    decay_log = head_decay.astype(jnp.float32).reshape(blocks, BLOCK, heads_here)
    steps_f = head_step.astype(jnp.float32).reshape(blocks, BLOCK, heads_here)
    running = jnp.cumsum(decay_log, axis=1)
    block_end = running[:, -1:, :]
    weighted_b = (
        keys_b.astype(jnp.float32) * (jnp.exp(block_end - running) * steps_f)[..., None]
    ).astype(jnp.bfloat16)
    block_states = jnp.einsum(
        "cshn,cshp->chnp", weighted_b, values, preferred_element_type=jnp.float32
    )
    block_gain = jnp.exp(block_end[:, 0, :])

    def advance(carried, inputs_now):
        state_now, decay_now = carried
        add_state, gain_now = inputs_now
        return (
            (gain_now[:, None, None] * state_now + add_state, decay_now * gain_now),
            (state_now, decay_now),
        )

    start_state = jnp.zeros((heads_here, N, P_SIZE), jnp.float32)
    start_decay = jnp.ones((heads_here,), jnp.float32)
    (section_state, section_decay), (local_entering, decay_before) = lax.scan(
        advance, (start_state, start_decay), (block_states, block_gain)
    )

    def relay_step(turn_index, incoming):
        outgoing = section_decay[:, None, None] * incoming + section_state
        return passed_along(outgoing, "sec", 1)

    carried_in = lax.fori_loop(
        0, lax.axis_size("sec") - 1, relay_step, jnp.zeros_like(section_state)
    )
    entering = local_entering + decay_before[:, :, None, None] * carried_in[None]
    skip_here = lax.dynamic_slice_in_dim(skip_gain, position * heads_here, heads_here, 0)
    causal_mask = lax.broadcasted_iota(jnp.int32, (BLOCK, BLOCK), 0) >= lax.broadcasted_iota(
        jnp.int32, (BLOCK, BLOCK), 1
    )

    def block_output(inputs_now):
        xblock, bblock, cblock, runblock, stepblock, stateblock = inputs_now
        scores = jnp.einsum("thn,shn->hts", cblock, bblock, preferred_element_type=jnp.float32)
        running_t = runblock.T
        log_gap = jnp.where(
            causal_mask[None], running_t[:, :, None] - running_t[:, None, :], -jnp.inf
        )
        mix_weights = (scores * jnp.exp(log_gap) * stepblock.T[:, None, :]).astype(jnp.bfloat16)
        within = jnp.einsum("hts,shp->thp", mix_weights, xblock, preferred_element_type=jnp.float32)
        carried_part = (
            jnp.einsum(
                "thn,hnp->thp",
                cblock.astype(jnp.float32),
                stateblock,
                precision=lax.Precision.HIGHEST,
                preferred_element_type=jnp.float32,
            )
            * jnp.exp(runblock)[:, :, None]
        )
        return (
            within + carried_part + skip_here[None, :, None] * xblock.astype(jnp.float32)
        ).astype(jnp.bfloat16)

    outputs = lax.map(block_output, (values, keys_b, query_c, running, steps_f, entering))
    outputs = outputs.reshape(section_rows, heads_here * P_SIZE)
    return lax.all_to_all(outputs, "cp", split_axis=0, concat_axis=1, tiled=True)


def solution(mesh):
    in_specs = (
        P(("sec", "cp"), None),
        P(),
        P(),
        P(("sec", "cp"), None),
        P(("sec", "cp"), None),
        P(),
    )
    out_specs = P(("sec", "cp"), None)
    return jax.shard_map(
        per_device, mesh=mesh, in_specs=in_specs, out_specs=out_specs, check_vma=False
    )
```

profile of v0, /device:TPU:0, one launch (start us, length us, event | category | flops | bytes accessed | tf_op | source)
XLA Modules:
  0.0 266.5 jit_solution(910163215070298945)
XLA Ops:
  1.0 4.8 %collective-permute-start.1 = (bf16[3,10240]{1,0:T(4,128)(2,1)S(1)}, bf16[3,10240]{1,0:T(4,128)(2,1)S(1)}, u32[]{:S(2)}, u32[]{:S(2)}) collective-permute-start(bf16[3,10240]{1,0:T(4,128)(2,1)S(1)} %slice.49), channel_id=1, source_target_pairs={{0,1},{1,2},{2,3},{3,4},{4,5},{5,6},{6,7},{7,8},{8,9},{9,10},{10,1... | collective-permute-start | bytes 184328 | tf_op jit(solution)/shard_map/ppermute | solution.py:17
  7.3 5.0 %all-to-all-start.2 = ((bf16[128,8,16]{0,2,1:T(8,128)(2,1)}), bf16[128,8,16]{0,2,1:T(8,128)(2,1)S(1)}, u32[]{:S(2)}, u32[]{:S(2)}) async-start(bf16[128,8,16]{0,2,1:T(8,128)(2,1)} %bitcast.12), calls=%async_computation.2 | async-start | bytes 65536 | tf_op jit(solution)/shard_map/all_to_all | solution.py:60
  13.7 4.4 %copy.52 = bf16[128,10240]{0,1:T(8,128)(2,1)} copy(bf16[128,10240]{1,0:T(8,128)(2,1)} %param.12) | data formatting | bytes 5242880 | tf_op args[0]
  20.9 15.0 %multiply_convert_fusion.2 = bf16[128,10240]{0,1:T(8,128)(2,1)S(1)} fusion(bf16[128,10240]{0,1:T(8,128)(2,1)} %copy.52, bf16[3,10240]{0,1:T(8,128)(2,1)} %copy.51, f32[10240]{0:T(1024)S(1)} %bitcast.141, f32[10240]{0:T(1024)S(1)} %bitcast.142, f32[10240]{0:T(1024)S(1)} %bitcast.140, f32[10240]{0:T(1024)S(1)} %bitcast.139, f32[10240]{0:T(1024)S(1)} %copy-done.4), kind=kLoop, calls=%fused_computation.41 | loop fusion | flops 34078720 | bytes 5509120 | tf_op jit(solution)/shard_map/convert_element_type | solution.py:28
  35.9 6.0 %all-to-all-start.3 = ((bf16[128,8,16]{0,2,1:T(8,128)(2,1)}), bf16[128,8,16]{0,2,1:T(8,128)(2,1)S(1)}, u32[]{:S(2)}, u32[]{:S(2)}) async-start(bf16[128,8,16]{0,2,1:T(8,128)(2,1)} %bitcast.17), calls=%async_computation.3 | async-start | bytes 65536 | tf_op jit(solution)/shard_map/all_to_all | solution.py:59
  42.8 5.9 %all-to-all-done.3 = bf16[128,8,16]{0,2,1:T(8,128)(2,1)S(1)} async-done(((bf16[128,8,16]{0,2,1:T(8,128)(2,1)}), bf16[128,8,16]{0,2,1:T(8,128)(2,1)S(1)}, u32[]{:S(2)}, u32[]{:S(2)}) %all-to-all-start.3) | async-done | bytes 32800 | tf_op jit(solution)/shard_map/all_to_all | solution.py:59
  48.6 3.5 %all-to-all-start.1 = ((bf16[128,8,256]{0,2,1:T(8,128)(2,1)}), bf16[128,8,256]{0,2,1:T(8,128)(2,1)S(1)}, u32[]{:S(2)}, u32[]{:S(2)}) async-start(bf16[128,8,256]{0,2,1:T(8,128)(2,1)} %pad_maximum_fusion.1), calls=%async_computation.1 | async-start | bytes 1048576 | tf_op jit(solution)/shard_map/all_to_all | solution.py:58
  53.6 12.1 %all-to-all-done.1 = bf16[128,8,256]{0,2,1:T(8,128)(2,1)S(1)} async-done(((bf16[128,8,256]{0,2,1:T(8,128)(2,1)}), bf16[128,8,256]{0,2,1:T(8,128)(2,1)S(1)}, u32[]{:S(2)}, u32[]{:S(2)}) %all-to-all-start.1) | async-done | bytes 524320 | tf_op jit(solution)/shard_map/all_to_all | solution.py:58
  66.6 3.8 %all-to-all-start = ((bf16[128,8,1024]{0,2,1:T(8,128)(2,1)}), bf16[128,8,1024]{0,2,1:T(8,128)(2,1)S(1)}, u32[]{:S(2)}, u32[]{:S(2)}) async-start(bf16[128,8,1024]{0,2,1:T(8,128)(2,1)} %bitcast.128), calls=%async_computation | async-start | bytes 4194304 | tf_op jit(solution)/shard_map/all_to_all | solution.py:57
  78.9 38.9 %all-to-all-done = bf16[128,8,1024]{0,2,1:T(8,128)(2,1)S(1)} async-done(((bf16[128,8,1024]{0,2,1:T(8,128)(2,1)}), bf16[128,8,1024]{0,2,1:T(8,128)(2,1)S(1)}, u32[]{:S(2)}, u32[]{:S(2)}) %all-to-all-start) | async-done | bytes 2097184 | tf_op jit(solution)/shard_map/all_to_all | solution.py:57
  120.5 3.1 %reshape.83 = bf16[4,256,16,64]{1,0,3,2:T(4,128)(2,1)S(1)} reshape(bf16[8,128,1024]{1,0,2:T(8,128)(2,1)} %copy.54) | data formatting | bytes 4194304 | tf_op jit(solution)/shard_map/reshape | solution.py:66
  125.4 6.5 %fusion.31 = f32[4,16,128,64]{3,2,1,0:T(8,128)} fusion(f32[4,256,16]{1,2,0:T(8,128)S(1)} %copy-done.3, f32[4,256,128]{2,1,0:T(8,128)S(1)} %copy-done.2, bf16[4,256,16,64]{1,0,3,2:T(4,128)(2,1)S(1)} %reshape.83), kind=kOutput, calls=%fused_computation.42 | convolution fusion | flops 272629760 | bytes 4784128 | tf_op jit(solution)/shard_map/cshn,cshp->chnp/dot_general | solution.py:80
  131.9 10.2 %while.40 = (s32[]{:T(128)}, f32[16,128,64]{2,1,0:T(8,128)S(1)}, f32[16]{0:T(128)S(1)}, f32[4,16,128,64]{3,2,1,0:T(8,128)}, f32[4,16]{1,0:T(4,128)S(1)}, /*index...) while((s32[]{:T(128)}, f32[16,128,64]{2,1,0:T(8,128)S(1)}, ...), condition=%wide.region_3.4_spmd.clone, body=%wide.region_2.3_spmd.clone.sunk | while | flops 524323 | bytes 3146869 | solution.py:95
  142.5 22.4 %while.38 = (s32[]{:T(128)}, f32[16,128,64]{1,2,0:T(8,128)S(1)}, f32[16]{0:T(128)S(1)}, f32[16,128,64]{1,2,0:T(8,128)S(1)}, s32[]{:T(128)}) while((s32[]{:T(128)}, f32[16,128,64]{1,2,0:T(8,128)S(1)}, f32[16]{0:T(128)S(1)}, f32[16,128,64]{1,2,0:T(8,128)S(1)}, s32[]{:T(128)}) %tuple.76), condition=%wide.region_5.6_spmd, body=%wide.region_4.5_spmd.sunk | while | flops 262146 | bytes 3670181 | solution.py:103
  145.5 7.2 %collective-permute-start = (f32[16,128,64]{1,2,0:T(8,128)S(1)}, f32[16,128,64]{1,2,0:T(8,128)S(1)}, u32[]{:S(2)}, u32[]{:S(2)}) collective-permute-start(f32[16,128,64]{1,2,0:T(8,128)S(1)} %multiply_add_fusion.3), channel_id=1, source_target_pairs={{0,8},{8,16},{16,24},{1,9},{9,17},{17,25},{2,10},{10,18},{18,26},{... | collective-permute-start | bytes 1572872 | tf_op jit(solution)/shard_map/while/body/eval_jaxpr/ppermute | solution.py:17
  154.4 9.0 %collective-permute-start = (f32[16,128,64]{1,2,0:T(8,128)S(1)}, f32[16,128,64]{1,2,0:T(8,128)S(1)}, u32[]{:S(2)}, u32[]{:S(2)}) collective-permute-start(f32[16,128,64]{1,2,0:T(8,128)S(1)} %multiply_add_fusion.3), channel_id=1, source_target_pairs={{0,8},{8,16},{16,24},{1,9},{9,17},{17,25},{2,10},{10,18},{18,26},{... | collective-permute-start | bytes 1572872 | tf_op jit(solution)/shard_map/while/body/eval_jaxpr/ppermute | solution.py:17
  165.2 4.6 %multiply_add_fusion.1 = f32[4,16,128,64]{3,2,1,0:T(8,128)} fusion(f32[4,16,128,64]{3,2,1,0:T(8,128)} %get-tuple-element.119, f32[16,128,64]{2,1,0:T(8,128)S(1)} %copy.69, f32[4,16]{1,0:T(4,128)S(1)} %get-tuple-element.120), kind=kLoop, calls=%fused_computation.43 | loop fusion | flops 1048576 | bytes 4718848 | tf_op jit(solution)/shard_map/add | solution.py:106
  169.8 2.9 %copy.72 = f32[4,16,128,64]{2,3,1,0:T(8,128)S(1)} copy(f32[4,16,128,64]{3,2,1,0:T(8,128)} %multiply_add_fusion.1) | data formatting | bytes 4194304
  172.7 3.0 %reshape.89 = bf16[4,256,16,128]{3,1,2,0:T(8,128)(2,1)} broadcast(bf16[4,256,128]{2,1,0:T(8,128)(2,1)S(1)} %bitcast.132), dimensions={0,1,3} | broadcast | bytes 4456448 | tf_op jit(solution)/shard_map/reshape | solution.py:67
  175.7 3.0 %reshape.87 = bf16[4,256,16,128]{3,1,2,0:T(8,128)(2,1)} broadcast(bf16[4,256,128]{2,1,0:T(8,128)(2,1)S(1)} %bitcast.135), dimensions={0,1,3} | broadcast | bytes 4456448 | tf_op jit(solution)/shard_map/reshape | solution.py:70
  178.7 27.1 %while.39 = (s32[]{:T(128)}, bf16[4,256,16,64]{1,3,2,0:T(8,128)(2,1)}, bf16[4,256,16,64]{1,3,2,0:T(8,128)(2,1)}, bf16[4,256,16,128]{3,1,2,0:T(8,128)(2,1)}, bf16...) while((s32[]{:T(128)}, ...), condition=%wide.region_7.8_spmd.clone, body=%wide.region_6.7_spmd.clone.sunk | while | flops 812187648 | bytes 7638637 | solution.py:135
  178.7 3.3 %fusion.56 = f32[256,16,64]{0,2,1:T(8,128)S(1)} fusion(f32[16,256]{1,0:T(8,128)S(1)} %get-tuple-element.413, f32[16,256]{1,0:T(8,128)S(1)} %get-tuple-element.414, pred[256,256]{1,0:T(8,128)(4,1)S(1)} %iota_compare_fusion.2, bf16[4,256,16,128]{3,1,2,0:T(8,128)(2,1)} %get-tuple-element.491, s32[]{:T(128)} %get-tuple-element.477, ...), kind=kOutput, calls=%fused_computation.4.clone.1 | convolution fusion | flops 407896064 | bytes 3786240 | tf_op jit(solution)/shard_map/while/body/eval_jaxpr/hts,shp->thp/dot_general | solution.py:120
  182.0 3.4 %fusion.57 = bf16[4,256,16,64]{1,3,2,0:T(8,128)(2,1)} fusion(bf16[4,256,16,64]{1,3,2,0:T(8,128)(2,1)} %get-tuple-element.478, s32[]{:T(128)} %get-tuple-element.477, f32[256,16,64]{0,2,1:T(8,128)S(1)} %fusion.56, bf16[4,256,16,128]{3,1,2,0:T(8,128)(2,1)} %get-tuple-element.490, f32[16]{0:T(128)S(1)} %get-tuple-element.495, ...), kind=kOutput, calls=%fused_computation.11.clone.1 | convolution fusion | flops 404226048 | bytes 3688448 | tf_op jit(solution)/shard_map/while/body/eval_jaxpr/thn,hnp->thp/dot_general | solution.py:122
  185.5 3.3 %fusion.56 = f32[256,16,64]{0,2,1:T(8,128)S(1)} fusion(f32[16,256]{1,0:T(8,128)S(1)} %get-tuple-element.413, f32[16,256]{1,0:T(8,128)S(1)} %get-tuple-element.414, pred[256,256]{1,0:T(8,128)(4,1)S(1)} %iota_compare_fusion.2, bf16[4,256,16,128]{3,1,2,0:T(8,128)(2,1)} %get-tuple-element.491, s32[]{:T(128)} %get-tuple-element.477, ...), kind=kOutput, calls=%fused_computation.4.clone.1 | convolution fusion | flops 407896064 | bytes 3786240 | tf_op jit(solution)/shard_map/while/body/eval_jaxpr/hts,shp->thp/dot_general | solution.py:120
  188.8 3.4 %fusion.57 = bf16[4,256,16,64]{1,3,2,0:T(8,128)(2,1)} fusion(bf16[4,256,16,64]{1,3,2,0:T(8,128)(2,1)} %get-tuple-element.478, s32[]{:T(128)} %get-tuple-element.477, f32[256,16,64]{0,2,1:T(8,128)S(1)} %fusion.56, bf16[4,256,16,128]{3,1,2,0:T(8,128)(2,1)} %get-tuple-element.490, f32[16]{0:T(128)S(1)} %get-tuple-element.495, ...), kind=kOutput, calls=%fused_computation.11.clone.1 | convolution fusion | flops 404226048 | bytes 3688448 | tf_op jit(solution)/shard_map/while/body/eval_jaxpr/thn,hnp->thp/dot_general | solution.py:122
  192.2 3.3 %fusion.56 = f32[256,16,64]{0,2,1:T(8,128)S(1)} fusion(f32[16,256]{1,0:T(8,128)S(1)} %get-tuple-element.413, f32[16,256]{1,0:T(8,128)S(1)} %get-tuple-element.414, pred[256,256]{1,0:T(8,128)(4,1)S(1)} %iota_compare_fusion.2, bf16[4,256,16,128]{3,1,2,0:T(8,128)(2,1)} %get-tuple-element.491, s32[]{:T(128)} %get-tuple-element.477, ...), kind=kOutput, calls=%fused_computation.4.clone.1 | convolution fusion | flops 407896064 | bytes 3786240 | tf_op jit(solution)/shard_map/while/body/eval_jaxpr/hts,shp->thp/dot_general | solution.py:120
  195.6 3.4 %fusion.57 = bf16[4,256,16,64]{1,3,2,0:T(8,128)(2,1)} fusion(bf16[4,256,16,64]{1,3,2,0:T(8,128)(2,1)} %get-tuple-element.478, s32[]{:T(128)} %get-tuple-element.477, f32[256,16,64]{0,2,1:T(8,128)S(1)} %fusion.56, bf16[4,256,16,128]{3,1,2,0:T(8,128)(2,1)} %get-tuple-element.490, f32[16]{0:T(128)S(1)} %get-tuple-element.495, ...), kind=kOutput, calls=%fused_computation.11.clone.1 | convolution fusion | flops 404226048 | bytes 3688448 | tf_op jit(solution)/shard_map/while/body/eval_jaxpr/thn,hnp->thp/dot_general | solution.py:122
  199.0 3.3 %fusion.56 = f32[256,16,64]{0,2,1:T(8,128)S(1)} fusion(f32[16,256]{1,0:T(8,128)S(1)} %get-tuple-element.413, f32[16,256]{1,0:T(8,128)S(1)} %get-tuple-element.414, pred[256,256]{1,0:T(8,128)(4,1)S(1)} %iota_compare_fusion.2, bf16[4,256,16,128]{3,1,2,0:T(8,128)(2,1)} %get-tuple-element.491, s32[]{:T(128)} %get-tuple-element.477, ...), kind=kOutput, calls=%fused_computation.4.clone.1 | convolution fusion | flops 407896064 | bytes 3786240 | tf_op jit(solution)/shard_map/while/body/eval_jaxpr/hts,shp->thp/dot_general | solution.py:120
  202.4 3.4 %fusion.57 = bf16[4,256,16,64]{1,3,2,0:T(8,128)(2,1)} fusion(bf16[4,256,16,64]{1,3,2,0:T(8,128)(2,1)} %get-tuple-element.478, s32[]{:T(128)} %get-tuple-element.477, f32[256,16,64]{0,2,1:T(8,128)S(1)} %fusion.56, bf16[4,256,16,128]{3,1,2,0:T(8,128)(2,1)} %get-tuple-element.490, f32[16]{0:T(128)S(1)} %get-tuple-element.495, ...), kind=kOutput, calls=%fused_computation.11.clone.1 | convolution fusion | flops 404226048 | bytes 3688448 | tf_op jit(solution)/shard_map/while/body/eval_jaxpr/thn,hnp->thp/dot_general | solution.py:122
  205.8 3.4 %copy.73 = bf16[4,256,16,64]{1,0,3,2:T(4,128)(2,1)S(1)} copy(bf16[4,256,16,64]{1,3,2,0:T(8,128)(2,1)} %get-tuple-element.124) | data formatting | bytes 4194304 | tf_op jit(solution)/shard_map/while | solution.py:135
  213.2 50.4 %all_to_all.77 = bf16[8,128,1024]{1,2,0:T(8,128)(2,1)S(1)} all-to-all(bf16[8,128,1024]{1,2,0:T(8,128)(2,1)S(1)} %copy.74), channel_id=1, replica_groups=mesh['sec'=4,'cp'=8] {'cp'}, dimensions={0} | all-to-all | bytes 4194304 | tf_op jit(solution)/shard_map/all_to_all | solution.py:137
  263.6 2.9 %copy.75 = bf16[128,8192]{1,0:T(8,128)(2,1)} copy(bf16[128,8192]{0,1:T(8,128)(2,1)S(1)} %bitcast.130) | data formatting | bytes 4194304 | tf_op jit(solution)/shard_map/all_to_all | solution.py:137
  (93 shorter events, 43.9 us)
Async XLA Ops:
  0.0 18.1 %copy-start.5 = (bf16[128,128]{1,0:T(8,128)(2,1)S(1)}, bf16[128,128]{1,0:T(8,128)(2,1)}, u32[]{:S(2)}) copy-start(bf16[128,128]{1,0:T(8,128)(2,1)} %param.15) | copy-start | bytes 98308
  1.0 17.8 %collective-permute-start.1 = (bf16[3,10240]{1,0:T(4,128)(2,1)S(1)}, bf16[3,10240]{1,0:T(4,128)(2,1)S(1)}, u32[]{:S(2)}, u32[]{:S(2)}) collective-permute-start(bf16[3,10240]{1,0:T(4,128)(2,1)S(1)} %slice.49), channel_id=1, source_target_pairs={{0,1},{1,2},{2,3},{3,4},{4,5},{5,6},{6,7},{7,8},{8,9},{9,10},{10,1... | collective-permute-start | bytes 184328 | tf_op jit(solution)/shard_map/ppermute | solution.py:17
  7.3 13.6 %copy-start.4 = (f32[10240]{0:T(1024)S(1)}, f32[10240]{0:T(1024)}, u32[]{:S(2)}) copy-start(f32[10240]{0:T(1024)} %param.14) | copy-start | bytes 122884
  7.3 28.6 %all-to-all-start.2 = ((bf16[128,8,16]{0,2,1:T(8,128)(2,1)}), bf16[128,8,16]{0,2,1:T(8,128)(2,1)S(1)}, u32[]{:S(2)}, u32[]{:S(2)}) async-start(bf16[128,8,16]{0,2,1:T(8,128)(2,1)} %bitcast.12), calls=%async_computation.2 | async-start | bytes 65536 | tf_op jit(solution)/shard_map/all_to_all | solution.py:60
  35.9 12.7 %all-to-all-start.3 = ((bf16[128,8,16]{0,2,1:T(8,128)(2,1)}), bf16[128,8,16]{0,2,1:T(8,128)(2,1)S(1)}, u32[]{:S(2)}, u32[]{:S(2)}) async-start(bf16[128,8,16]{0,2,1:T(8,128)(2,1)} %bitcast.17), calls=%async_computation.3 | async-start | bytes 65536 | tf_op jit(solution)/shard_map/all_to_all | solution.py:59
  48.6 17.1 %all-to-all-start.1 = ((bf16[128,8,256]{0,2,1:T(8,128)(2,1)}), bf16[128,8,256]{0,2,1:T(8,128)(2,1)S(1)}, u32[]{:S(2)}, u32[]{:S(2)}) async-start(bf16[128,8,256]{0,2,1:T(8,128)(2,1)} %pad_maximum_fusion.1), calls=%async_computation.1 | async-start | bytes 1048576 | tf_op jit(solution)/shard_map/all_to_all | solution.py:58
  52.1 18.3 %copy-start.6 = (f32[128]{0:T(128)S(1)}, f32[128]{0:T(128)}, u32[]{:S(2)}) copy-start(f32[128]{0:T(128)} %param.17) | copy-start | bytes 1540
  65.8 0.8 copy-start
  66.6 51.2 %all-to-all-start = ((bf16[128,8,1024]{0,2,1:T(8,128)(2,1)}), bf16[128,8,1024]{0,2,1:T(8,128)(2,1)S(1)}, u32[]{:S(2)}, u32[]{:S(2)}) async-start(bf16[128,8,1024]{0,2,1:T(8,128)(2,1)} %bitcast.128), calls=%async_computation | async-start | bytes 4194304 | tf_op jit(solution)/shard_map/all_to_all | solution.py:57
  123.6 1.8 copy-start.2
  123.6 1.8 copy-start.3
  142.6 2.8 %collective-permute-start = (f32[16,128,64]{1,2,0:T(8,128)S(1)}, f32[16,128,64]{1,2,0:T(8,128)S(1)}, u32[]{:S(2)}, u32[]{:S(2)}) collective-permute-start(f32[16,128,64]{1,2,0:T(8,128)S(1)} %multiply_add_fusion.3), channel_id=1, source_target_pairs={{0,8},{8,16},{16,24},{1,9},{9,17},{17,25},{2,10},{10,18},{18,26},{... | collective-permute-start | bytes 1572872 | tf_op jit(solution)/shard_map/while/body/eval_jaxpr/ppermute | solution.py:17
  145.5 8.7 %collective-permute-start = (f32[16,128,64]{1,2,0:T(8,128)S(1)}, f32[16,128,64]{1,2,0:T(8,128)S(1)}, u32[]{:S(2)}, u32[]{:S(2)}) collective-permute-start(f32[16,128,64]{1,2,0:T(8,128)S(1)} %multiply_add_fusion.3), channel_id=1, source_target_pairs={{0,8},{8,16},{16,24},{1,9},{9,17},{17,25},{2,10},{10,18},{18,26},{... | collective-permute-start | bytes 1572872 | tf_op jit(solution)/shard_map/while/body/eval_jaxpr/ppermute | solution.py:17
  154.4 10.5 %collective-permute-start = (f32[16,128,64]{1,2,0:T(8,128)S(1)}, f32[16,128,64]{1,2,0:T(8,128)S(1)}, u32[]{:S(2)}, u32[]{:S(2)}) collective-permute-start(f32[16,128,64]{1,2,0:T(8,128)S(1)} %multiply_add_fusion.3), channel_id=1, source_target_pairs={{0,8},{8,16},{16,24},{1,9},{9,17},{17,25},{2,10},{10,18},{18,26},{... | collective-permute-start | bytes 1572872 | tf_op jit(solution)/shard_map/while/body/eval_jaxpr/ppermute | solution.py:17
  169.8 5.9 %copy-start.1 = (bf16[1024,128]{1,0:T(8,128)(2,1)S(1)}, bf16[1024,128]{1,0:T(8,128)(2,1)}, u32[]{:S(2)}) copy-start(bf16[1024,128]{1,0:T(8,128)(2,1)} %get-tuple-element.285) | copy-start | bytes 786436
where the time goes:
time: 270 us; the launch traced here: 266 us
  waiting for transfers between devices  61.3 us (23%)
  blocking collectives  50.4 us (19%)
  local copies, waits for them, and re-layouts  45.5 us (17%)
  starting transfers between devices  40.7 us (15%)
  other arithmetic  34.8 us (13%)
  matrix products  33.3 us (12%)
    all_to_all x1, blocking collectives, per_device(): lax.all_to_all(outputs, 'cp', split_axis=0, concat_axis=1, tiled=True)  50.4 us
    all_to_all x1, waiting for transfers between devices, per_device(): lax.all_to_all(mixed_cols[:, :width_x], 'cp', split_axis=1, concat_axis=0...  38.9 us
    ppermute x4, starting transfers between devices, passed_along(): lax.ppermute(value, axis, [(source, source + steps) for source in range(l...  22.4 us
    convert_element_type x1, other arithmetic, causal_conv(): return jax.nn.silu(summed).astype(jnp.bfloat16)  15 us
    dot_general x4, matrix products, block_output(): jnp.einsum('thn,hnp->thp', cblock.astype(jnp.float32), stateblock, precis...  13.5 us
    dot_general x4, matrix products, block_output(): jnp.einsum('hts,shp->thp', mix_weights, xblock, preferred_element_type=jn...  13.3 us
    all_to_all x1, waiting for transfers between devices, per_device(): lax.all_to_all(send_bc, 'cp', split_axis=1, concat_axis=0, tiled=True)  12.1 us
    unnamed x19, local copies, waits for them, and re-layouts  12.1 us
  transfers between devices with their start and end apart: 8, of which 6 were waited for; matrix products, arithmetic and copies ran while one was open for 13% of the time, Pallas kernels for 0%

commit v1 on v0

v1 whole, which is shorter than its diff:
```python
import functools
import jax
import jax.numpy as jnp
from jax import lax
from jax.experimental import pallas as pl
from jax.experimental.pallas import tpu as pltpu
from jax.sharding import PartitionSpec as P

HEAD_COUNT = 128
P_SIZE = 64
N = 128
G = 8
KERNEL = 4
GROUP_HEADS = HEAD_COUNT // G
GROUP_COLS = GROUP_HEADS * P_SIZE
WIDTH_X = HEAD_COUNT * P_SIZE
RIM = 8
VMEM_LIMIT = 48 * 1024 * 1024


def passed_along(value, axis, steps):
    count = lax.axis_size(axis)
    return lax.ppermute(value, axis, [(source, source + steps) for source in range(count - steps)])


def conv_silu(block_ref, rim_ref, weight_ref, bias_ref):
    now = block_ref[...].astype(jnp.float32)
    rim = rim_ref[...].astype(jnp.float32)
    row = lax.broadcasted_iota(jnp.int32, rim.shape, 0)
    total = bias_ref[...] + weight_ref[KERNEL - 1 : KERNEL, :] * now
    for back in range(1, KERNEL):
        moved = pltpu.roll(now, back, 0)
        top = jnp.where(row < back, pltpu.roll(rim, back, 0), moved[:RIM])
        moved = jnp.concatenate([top, moved[RIM:]], 0)
        total = total + weight_ref[KERNEL - 1 - back : KERNEL - back, :] * moved
    return (total / (1.0 + jnp.exp(-total))).astype(jnp.bfloat16)


def spread(columns, pair):
    rows = columns.shape[0]
    lane = lax.broadcasted_iota(jnp.int32, (rows, 2 * P_SIZE), 1)
    return jnp.where(lane < P_SIZE, columns[:, 2 * pair : 2 * pair + 1], columns[:, 2 * pair + 1 : 2 * pair + 2])


def conv_state_kernel(
    px, pb, pc, rx, rb, rc, wx, wb, wc, bx, bb, bc, run_ref, step_ref,
    x_out, b_out, c_out, state_out,
):
    x = conv_silu(px, rx, wx, bx)
    b = conv_silu(pb, rb, wb, bb)
    x_out[...] = x
    b_out[...] = b
    c_out[...] = conv_silu(pc, rc, wc, bc)
    run = run_ref[0]
    scale = jnp.exp(run[-1:, :] - run) * step_ref[0]
    parts = []
    for pair in range(GROUP_HEADS // 2):
        columns = x[:, pair * 2 * P_SIZE : (pair + 1) * 2 * P_SIZE].astype(jnp.float32)
        parts.append((columns * spread(scale, pair)).astype(jnp.bfloat16))
    weighted = jnp.concatenate(parts, 1)
    state = lax.dot_general(
        b, weighted, (((0,), (0,)), ((), ())), preferred_element_type=jnp.float32
    ).astype(jnp.bfloat16)
    pieces, _, width = state_out.shape
    for piece in range(pieces):
        state_out[piece] = state[:, piece * width : (piece + 1) * width]


def within_kernel(x_ref, b_ref, c_ref, run_ref, run_row_ref, step_row_ref, skip_ref, out_ref):
    rows = x_ref.shape[0]
    scores = lax.dot_general(
        c_ref[...], b_ref[...], (((1,), (1,)), ((), ())), preferred_element_type=jnp.float32
    )
    token = lax.broadcasted_iota(jnp.int32, (rows, rows), 0)
    source = lax.broadcasted_iota(jnp.int32, (rows, rows), 1)
    scores = jnp.where(token >= source, scores, 0.0)
    run = run_ref[0]
    lane = lax.broadcasted_iota(jnp.int32, (rows, 2 * P_SIZE), 1)
    for pair in range(GROUP_HEADS // 2):
        columns = slice(pair * 2 * P_SIZE, (pair + 1) * 2 * P_SIZE)
        x = x_ref[:, columns]
        found = []
        for head in (2 * pair, 2 * pair + 1):
            gap = run[:, head : head + 1] - run_row_ref[head : head + 1, :]
            mix = scores * jnp.exp(jnp.minimum(gap, 0.0)) * step_row_ref[head : head + 1, :]
            found.append(jnp.dot(mix.astype(jnp.bfloat16), x, preferred_element_type=jnp.float32))
        out_ref[:, columns] = (
            jnp.where(lane < P_SIZE, found[0], found[1]) + skip_ref[:, columns] * x.astype(jnp.float32)
        )


def total_kernel(state_ref, gain_ref, total_ref):
    total = state_ref[0].astype(jnp.float32)
    for piece in range(1, state_ref.shape[0]):
        total = gain_ref[piece : piece + 1, :] * total + state_ref[piece].astype(jnp.float32)
    total_ref[...] = total


def entering_kernel(state_ref, gain_ref, totals_ref, coef_ref, out_ref):
    now = coef_ref[0:1, :] * totals_ref[0]
    for section in range(1, totals_ref.shape[0]):
        now = now + coef_ref[section : section + 1, :] * totals_ref[section]
    for piece in range(state_ref.shape[0]):
        out_ref[piece] = now.astype(jnp.bfloat16)
        now = gain_ref[piece : piece + 1, :] * now + state_ref[piece].astype(jnp.float32)


def finish_kernel(within_ref, c_ref, run_ref, enter_ref, out_ref):
    pieces = enter_ref.shape[0]
    enter = jnp.concatenate([enter_ref[piece] for piece in range(pieces)], 1) if pieces > 1 else enter_ref[0]
    carried = jnp.dot(c_ref[...], enter, preferred_element_type=jnp.float32)
    gain = jnp.exp(run_ref[0])
    for pair in range(GROUP_HEADS // 2):
        columns = slice(pair * 2 * P_SIZE, (pair + 1) * 2 * P_SIZE)
        out_ref[:, columns] = (
            within_ref[:, columns] + spread(gain, pair) * carried[:, columns]
        ).astype(jnp.bfloat16)


def params():
    return pltpu.CompilerParams(vmem_limit_bytes=VMEM_LIMIT)


def per_device(projected, conv_weight, conv_bias, step_size, log_decay, skip_gain):
    sections = lax.axis_size("sec")
    targets = lax.axis_size("cp")
    section = lax.axis_index("sec")
    position = lax.axis_index("cp")
    rows = projected.shape[0]
    width = WIDTH_X // targets
    pieces = GROUP_COLS // width
    heads_here = HEAD_COUNT // targets
    rim = passed_along(projected[rows - RIM :], ("sec", "cp"), 1)
    lower = jnp.tril(jnp.ones((rows, rows), jnp.bfloat16))
    running = jnp.dot(lower, log_decay, preferred_element_type=jnp.float32)
    run_row = running.T
    run_cols = running.reshape(rows, G, GROUP_HEADS).transpose(1, 0, 2)
    steps_f = step_size.astype(jnp.float32)
    step_row = steps_f.T
    step_cols = steps_f.reshape(rows, G, GROUP_HEADS).transpose(1, 0, 2)
    skip_cols = jnp.repeat(skip_gain, P_SIZE)[None]
    bias = conv_bias[None]
    ends = lax.all_gather(running[rows - 1 :], ("sec", "cp"), axis=0, tiled=True)
    ends = ends.reshape(sections, targets, HEAD_COUNT)
    ends = lax.dynamic_slice_in_dim(ends, position * heads_here, heads_here, 2)
    mine = lax.dynamic_slice_in_dim(ends, section, 1, 0)[0]
    gain = jnp.repeat(jnp.exp(mine), P_SIZE, axis=1)
    through = jnp.cumsum(jnp.sum(ends, 1), axis=0)
    before = jnp.where(section > 0, lax.dynamic_slice_in_dim(through, jnp.maximum(section - 1, 0), 1, 0), 0.0)
    earlier = lax.broadcasted_iota(jnp.int32, through.shape, 0) < section
    coef = jnp.where(earlier, jnp.exp(jnp.minimum(before - through, 0.0)), 0.0)
    coef = jnp.repeat(coef, P_SIZE, axis=1)

    def spec(height, cols, first):
        return pl.BlockSpec((height, cols), lambda g: (0, first + g))

    def three(height):
        return [spec(height, GROUP_COLS, 0), spec(height, N, WIDTH_X // N), spec(height, N, WIDTH_X // N + G)]

    group_cols = pl.BlockSpec((1, rows, GROUP_HEADS), lambda g: (g, 0, 0))
    group_rows = pl.BlockSpec((GROUP_HEADS, rows), lambda g: (g, 0))
    piece_spec = pl.BlockSpec((pieces, N, width), lambda g: (g, 0, 0))
    x, b, c, state = pl.pallas_call(
        conv_state_kernel,
        grid=(G,),
        in_specs=three(rows) + three(RIM) + three(KERNEL) + three(1) + [group_cols, group_cols],
        out_specs=[spec(rows, GROUP_COLS, 0), spec(rows, N, 0), spec(rows, N, 0), piece_spec],
        out_shape=[
            jax.ShapeDtypeStruct((rows, WIDTH_X), jnp.bfloat16),
            jax.ShapeDtypeStruct((rows, G * N), jnp.bfloat16),
            jax.ShapeDtypeStruct((rows, G * N), jnp.bfloat16),
            jax.ShapeDtypeStruct((targets, N, width), jnp.bfloat16),
        ],
        compiler_params=params(),
        name="conv_state",
    )(*([projected] * 3), *([rim] * 3), *([conv_weight] * 3), *([bias] * 3), run_cols, step_cols)
    state = lax.all_to_all(state, "cp", split_axis=0, concat_axis=0, tiled=True)
    within = pl.pallas_call(
        within_kernel,
        grid=(G,),
        in_specs=[spec(rows, GROUP_COLS, 0), spec(rows, N, 0), spec(rows, N, 0), group_cols, group_rows, group_rows, spec(1, GROUP_COLS, 0)],
        out_specs=spec(rows, GROUP_COLS, 0),
        out_shape=jax.ShapeDtypeStruct((rows, WIDTH_X), jnp.float32),
        compiler_params=params(),
        cost_estimate=pl.CostEstimate(flops=2 * 2 * HEAD_COUNT * rows * rows * N, bytes_accessed=8 * 1024 * 1024, transcendentals=HEAD_COUNT * rows * rows),
        name="within",
    )(x, b, c, run_cols, run_row, step_row, skip_cols)
    total = pl.pallas_call(
        total_kernel,
        out_shape=jax.ShapeDtypeStruct((N, width), jnp.float32),
        compiler_params=params(),
        name="section_total",
    )(state, gain)
    totals = lax.all_gather(total, "sec", axis=0)
    entering = pl.pallas_call(
        entering_kernel,
        out_shape=jax.ShapeDtypeStruct((targets, N, width), jnp.bfloat16),
        compiler_params=params(),
        name="entering",
    )(state, gain, totals, coef)
    entering = lax.all_to_all(entering, "cp", split_axis=0, concat_axis=0, tiled=True)
    return pl.pallas_call(
        finish_kernel,
        grid=(G,),
        in_specs=[spec(rows, GROUP_COLS, 0), spec(rows, N, 0), group_cols, piece_spec],
        out_specs=spec(rows, GROUP_COLS, 0),
        out_shape=jax.ShapeDtypeStruct((rows, WIDTH_X), jnp.bfloat16),
        compiler_params=params(),
        name="finish",
    )(within, c, run_cols, entering)


def solution(mesh):
    in_specs = (
        P(("sec", "cp"), None),
        P(),
        P(),
        P(("sec", "cp"), None),
        P(("sec", "cp"), None),
        P(),
    )
    out_specs = P(("sec", "cp"), None)
    return jax.shard_map(
        per_device, mesh=mesh, in_specs=in_specs, out_specs=out_specs, check_vma=False
    )
```

time: 270 us -> 232 us (0.86); the launches traced: 266 us -> 232 us
  blocking collectives: 50.4 us -> 104 us
  local copies, waits for them, and re-layouts: 45.5 us -> 10.1 us
  other arithmetic: 34.8 us -> 0.22 us
  matrix products: 33.3 us -> 0.13 us
  Pallas kernels: 0 us -> 25 us
  starting transfers between devices: 40.7 us -> 17.3 us
  between operations: 0.27 us -> 13.5 us
    all_gather x0 -> x1, blocking collectives: none -> 104 us  [per_device(): ends = lax.all_gather(running[rows - 1:], ('sec', 'cp'), axis=0, tiled=True)]
    all_to_all x1 -> x0, blocking collectives: 50.4 us -> none  [per_device(): lax.all_to_all(outputs, 'cp', split_axis=0, concat_axis=1, tiled=True)]
    dot_general x9 -> x1, matrix products: 33.3 us -> 0.13 us  [per_device(): running = jnp.dot(lower, log_decay, preferred_element_type=jnp.float32)]
    pallas_call x0 -> x5, Pallas kernels: none -> 25 us  [the longest x1 7.9 us: per_device(): pl.pallas_call(conv_state_kernel, grid=(G,), in_specs=three(rows) + three...]
    all_gather x0 -> x1, waiting for transfers between devices: none -> 18.7 us  [per_device(): totals = lax.all_gather(total, 'sec', axis=0)]
    ppermute x4 -> x1, starting transfers between devices: 22.4 us -> 4.85 us  [passed_along(): lax.ppermute(value, axis, [(source, source + steps) for source in range(c...]
    all_to_all x4 -> x2, waiting for transfers between devices: 56.9 us -> 40.5 us  [the longest x1 40.5 us: per_device(): lax.all_to_all(entering, 'cp', split_axis=0, concat_axis=0, tiled=True)]
    convert_element_type x3 -> x0, other arithmetic: 15.8 us -> none  [the longest x1 15 us: causal_conv(): return jax.nn.silu(summed).astype(jnp.bfloat16)]
  transfers between devices with their start and end apart: 8 -> 4, of which waited for: 6 -> 3; matrix products, arithmetic and copies ran while one was open for 13% -> 1% of each run, Pallas kernels for 0% -> 3%
where the time goes in v1:
time: 232 us
  blocking collectives  104 us (45%)
  waiting for transfers between devices  61.2 us (26%)
  Pallas kernels  25 us (11%)
  starting transfers between devices  17.3 us (7%)
  between operations  13.5 us (6%)
  local copies, waits for them, and re-layouts  10.1 us (4%)
    all_gather x1, blocking collectives, per_device(): ends = lax.all_gather(running[rows - 1:], ('sec', 'cp'), axis=0, tiled=True)  104 us
    all_to_all x1, waiting for transfers between devices, per_device(): lax.all_to_all(entering, 'cp', split_axis=0, concat_axis=0, tiled=True)  40.5 us
    all_gather x1, waiting for transfers between devices, per_device(): totals = lax.all_gather(total, 'sec', axis=0)  18.7 us
    unnamed x18, local copies, waits for them, and re-layouts  8.12 us
    pallas_call x1, Pallas kernels, per_device(): pl.pallas_call(conv_state_kernel, grid=(G,), in_specs=three(rows) + three...  7.9 us
    pallas_call x1, Pallas kernels, per_device(): pl.pallas_call(finish_kernel, grid=(G,), in_specs=[spec(rows, GROUP_COLS,...  7.48 us
    all_to_all x1, starting transfers between devices, per_device(): state = lax.all_to_all(state, 'cp', split_axis=0, concat_axis=0, tiled=True)  6.8 us
    pallas_call x1, Pallas kernels, per_device(): pl.pallas_call(within_kernel, grid=(G,), in_specs=[spec(rows, GROUP_COLS,...  6.29 us
  transfers between devices with their start and end apart: 4, of which 3 were waited for; matrix products, arithmetic and copies ran while one was open for 1% of the time, Pallas kernels for 3%

profile of v1, /device:TPU:0, one launch (start us, length us, event | category | flops | bytes accessed | tf_op | source)
XLA Modules:
  0.0 231.5 jit_solution(15507376391925953839)
XLA Ops:
  6.5 0.9 slice.6
  7.5 4.9 %collective-permute-start = (bf16[8,10240]{1,0:T(8,128)(2,1)S(1)}, bf16[8,10240]{1,0:T(8,128)(2,1)S(1)}, u32[]{:S(2)}, u32[]{:S(2)}) collective-permute-start(bf16[8,10240]{1,0:T(8,128)(2,1)S(1)} %slice.6), channel_id=1, source_target_pairs={{0,1},{1,2},{2,3},{3,4},{4,5},{5,6},{6,7},{7,8},{8,9},{9,10},{10,1... | collective-permute-start | bytes 491528 | tf_op jit(solution)/shard_map/ppermute | solution.py:23
  12.3 0.1 fusion.1
  12.5 0.1 copy.15
  12.6 0.2 copy.16
  12.8 0.9 copy.17
  13.7 0.2 copy.18
  13.8 1.9 collective-permute-done.rx.rb.rc
  15.8 0.9 copy-done.5
  16.7 0.8 copy-done.6
  17.5 7.9 %conv_state.1 = (bf16[128,8192]{1,0:T(8,128)(2,1)S(1)}, bf16[128,1024]{1,0:T(8,128)(2,1)S(1)}, bf16[128,1024]{1,0:T(8,128)(2,1)S(1)}, bf16[8,128,1024]{2,1,0:T(8,128)(2,1)S(1)}) custom-call(bf16[128,10240]{1,0:T(8,128)(2,1)} %pc.1, bf16[128,10240]{1,0:T(8,128)(2,1)} %pc.1, bf16[128,10240]{1,0:T(8,128)(2,1)} %pc.1, ...), custom_call_target="tpu_custom_call" | custom-call | tf_op jit(solution)/shard_map/conv_state/pallas_call | solution.py:163
  25.4 1.3 copy-done.2
  26.7 1.3 copy-done.4
  28.0 6.8 %all-to-all-start = ((bf16[8,128,1024]{2,1,0:T(8,128)(2,1)}), bf16[8,128,1024]{2,1,0:T(8,128)(2,1)S(1)}, u32[]{:S(2)}, u32[]{:S(2)}) async-start(bf16[8,128,1024]{2,1,0:T(8,128)(2,1)} %copy-done.4), calls=%async_computation | async-start | bytes 4194304 | tf_op jit(solution)/shard_map/all_to_all | solution.py:177
  34.9 104.0 %all-gather.1 = f32[32,1,128]{2,1,0:T(1,128)S(1)} all-gather(f32[1,1,128]{2,1,0:T(1,128)S(1)} %slice_bitcast_fusion), channel_id=1, replica_groups=mesh['sec'=4,'cp'=8] {'sec','cp'}, dimensions={0}, use_global_device_ids=true | all-gather | bytes 16896 | tf_op jit(solution)/shard_map/all_gather | solution.py:143
  138.9 0.1 exponential_bitcast_fusion
  139.0 0.1 broadcast_in_dim.29
  139.1 0.1 reshape.19.gain_ref
  139.2 1.2 section_total.1
  140.4 0.1 dynamic-slice_reduce_fusion
  140.6 0.1 broadcast_in_dim.31
  140.7 0.1 reshape.20.coef_ref
  140.8 18.7 %all-gather.4.cloned.1.call-done = f32[512,1024]{1,0:T(8,128)} async-done(((f32[128,1024]{1,0:T(8,128)}), f32[512,1024]{1,0:T(8,128)}) %all-gather.4.cloned.1.call-update) | async-done | bytes 2097168 | tf_op jit(solution)/shard_map/all_gather | solution.py:194
  159.4 2.2 entering.1
  161.6 1.3 copy-done.1
  162.9 5.6 %all-to-all-start.1 = ((bf16[8,128,1024]{2,1,0:T(8,128)(2,1)}), bf16[8,128,1024]{2,1,0:T(8,128)(2,1)S(1)}, u32[]{:S(2)}, u32[]{:S(2)}) async-start(bf16[8,128,1024]{2,1,0:T(8,128)(2,1)} %copy-done.1), calls=%async_computation.1 | async-start | bytes 4194304 | tf_op jit(solution)/shard_map/all_to_all | solution.py:201
  168.6 0.1 broadcast_in_dim.28
  168.6 0.1 broadcast_in_dim_reshape.3.skip_ref
  168.8 1.6 copy-done.3
  170.4 6.3 %within.1.within_ref = f32[128,8192]{1,0:T(8,128)} custom-call(bf16[128,8192]{1,0:T(8,128)(2,1)S(1)} %copy-done.3, bf16[128,1024]{1,0:T(8,128)(2,1)S(1)} %get-tuple-element.10.b_ref, bf16[128,1024]{1,0:T(8,128)(2,1)S(1)} %get-tuple-element.11.c_ref, f32[8,128,16]{2,1,0:T(8,128)S(1)} %bitcast.19, f32[128,128]{1,0:T(8,128)S(1)} %bitcast.23, ...), custom_call_target="tpu_custom_call" | custom-call | flops 1073741824 | bytes 8388608 | tf_op jit(solution)/shard_map/within/pallas_call | solution.py:178
  176.7 40.5 %all-to-all-done.1.enter_ref = bf16[8,128,1024]{2,1,0:T(8,128)(2,1)S(1)} async-done(((bf16[8,128,1024]{2,1,0:T(8,128)(2,1)}), bf16[8,128,1024]{2,1,0:T(8,128)(2,1)S(1)}, u32[]{:S(2)}, u32[]{:S(2)}) %all-to-all-start.1) | async-done | bytes 2097184 | tf_op jit(solution)/shard_map/all_to_all | solution.py:201
  217.2 7.5 %finish.1 = bf16[128,8192]{1,0:T(8,128)(2,1)} custom-call(f32[128,8192]{1,0:T(8,128)} %within.1.within_ref, bf16[128,1024]{1,0:T(8,128)(2,1)S(1)} %get-tuple-element.11.c_ref, f32[8,128,16]{2,1,0:T(8,128)S(1)} %bitcast.20, bf16[8,128,1024]{2,1,0:T(8,128)(2,1)S(1)} %all-to-all-done.1.enter_ref), custom_call_target="tpu_custom_call" | custom-call | tf_op jit(solution)/shard_map/finish/pallas_call | solution.py:202
  (19 shorter events, 0.2 us)
Async XLA Ops:
  6.5 5.8 %copy-start = (bf16[128,128]{1,0:T(8,128)(2,1)S(1)}, bf16[128,128]{1,0:T(8,128)(2,1)}, u32[]{:S(2)}) copy-start(bf16[128,128]{1,0:T(8,128)(2,1)} %param.10) | copy-start | bytes 98308
  7.5 8.3 %collective-permute-start = (bf16[8,10240]{1,0:T(8,128)(2,1)S(1)}, bf16[8,10240]{1,0:T(8,128)(2,1)S(1)}, u32[]{:S(2)}, u32[]{:S(2)}) collective-permute-start(bf16[8,10240]{1,0:T(8,128)(2,1)S(1)} %slice.6), channel_id=1, source_target_pairs={{0,1},{1,2},{2,3},{3,4},{4,5},{5,6},{6,7},{7,8},{8,9},{9,10},{10,1... | collective-permute-start | bytes 491528 | tf_op jit(solution)/shard_map/ppermute | solution.py:23
  15.8 0.9 copy-start.5
  16.7 0.8 copy-start.6
  25.4 1.3 copy-start.2
  26.7 1.3 copy-start.4
  28.0 111.1 %all-to-all-start = ((bf16[8,128,1024]{2,1,0:T(8,128)(2,1)}), bf16[8,128,1024]{2,1,0:T(8,128)(2,1)S(1)}, u32[]{:S(2)}, u32[]{:S(2)}) async-start(bf16[8,128,1024]{2,1,0:T(8,128)(2,1)} %copy-done.4), calls=%async_computation | async-start | bytes 4194304 | tf_op jit(solution)/shard_map/all_to_all | solution.py:177
  34.8 124.6 %all-gather.4.cloned.1.call-start = ((), (), s32[]{:S(2)}) async-start(), calls=%async_computation.2 | async-start | bytes 2621440 | tf_op jit(solution)/shard_map/all_gather | solution.py:194
  161.6 1.3 copy-start.1
  162.9 5.6 %copy-start.7 = (f32[128]{0:T(128)S(1)}, f32[128]{0:T(128)}, u32[]{:S(2)}) copy-start(f32[128]{0:T(128)} %param.11) | copy-start | bytes 1540
  162.9 54.3 %all-to-all-start.1 = ((bf16[8,128,1024]{2,1,0:T(8,128)(2,1)}), bf16[8,128,1024]{2,1,0:T(8,128)(2,1)S(1)}, u32[]{:S(2)}, u32[]{:S(2)}) async-start(bf16[8,128,1024]{2,1,0:T(8,128)(2,1)} %copy-done.1), calls=%async_computation.1 | async-start | bytes 4194304 | tf_op jit(solution)/shard_map/all_to_all | solution.py:201
  168.8 1.6 copy-start.3
Sparse Core Ops, SparseCore 0:
  140.5 18.9 all-gather.3

commit v2 on v1

--- a/solution.py
+++ b/solution.py
@@ -15,6 +15,7 @@
 GROUP_COLS = GROUP_HEADS * P_SIZE
 WIDTH_X = HEAD_COUNT * P_SIZE
 RIM = 8
+CHUNKS = 4
 VMEM_LIMIT = 48 * 1024 * 1024
 
 
@@ -61,9 +62,11 @@
     state = lax.dot_general(
         b, weighted, (((0,), (0,)), ((), ())), preferred_element_type=jnp.float32
     ).astype(jnp.bfloat16)
-    pieces, _, width = state_out.shape
-    for piece in range(pieces):
-        state_out[piece] = state[:, piece * width : (piece + 1) * width]
+    _, chunks, places, _, width = state_out.shape
+    for place in range(places):
+        for chunk in range(chunks):
+            begin = (place * chunks + chunk) * width
+            state_out[0, chunk, place] = state[:, begin : begin + width]
 
 
 def within_kernel(x_ref, b_ref, c_ref, run_ref, run_row_ref, step_row_ref, skip_ref, out_ref):
@@ -89,25 +92,153 @@
         )
 
 
-def total_kernel(state_ref, gain_ref, total_ref):
-    total = state_ref[0].astype(jnp.float32)
-    for piece in range(1, state_ref.shape[0]):
-        total = gain_ref[piece : piece + 1, :] * total + state_ref[piece].astype(jnp.float32)
-    total_ref[...] = total
-
-
-def entering_kernel(state_ref, gain_ref, totals_ref, coef_ref, out_ref):
-    now = coef_ref[0:1, :] * totals_ref[0]
-    for section in range(1, totals_ref.shape[0]):
-        now = now + coef_ref[section : section + 1, :] * totals_ref[section]
-    for piece in range(state_ref.shape[0]):
-        out_ref[piece] = now.astype(jnp.bfloat16)
-        now = gain_ref[piece : piece + 1, :] * now + state_ref[piece].astype(jnp.float32)
+def scan_kernel(
+    state_ref, gain_ref, out_ref,
+    from_pair, block_send, block_recv, total_send, total_recv, enter_send, enter_recv, back_send,
+    pair_gain, block_gain, block_gains, section_gain, section_gains,
+    pair_sems, block_sems, total_sems, enter_sems, back_sems, pair_gain_sems, block_gain_sems, section_gain_sems,
+):
+    sections = lax.axis_size("sec")
+    section, position = lax.axis_index("sec"), lax.axis_index("cp")
+    place, side = position // 2, position % 2
+    _, chunks, places, rows, width = state_ref.shape
+    first = side == 0
+    partner = (section, place * 2 + (1 - side))
+    near = [lax.rem(place + step, places) for step in range(1, places)]
+    line = [(section, other * 2 + side) for other in near]
+    above = [(lax.rem(section + step, sections), position) for step in range(1, sections)]
+
+    def remote(source, target, sems, at, device):
+        return pltpu.make_async_remote_copy(
+            src_ref=source,
+            dst_ref=target,
+            send_sem=sems.at[(0, *at)],
+            recv_sem=sems.at[(1, *at)],
+            device_id=device,
+            device_id_type=pl.DeviceIdType.MESH,
+        )
+
+    barrier = pltpu.get_barrier_semaphore()
+    for device in [partner, *line, *above]:
+        pl.semaphore_signal(barrier, inc=1, device_id=device, device_id_type=pl.DeviceIdType.MESH)
+    pl.semaphore_wait(barrier, len(line) + len(above) + 1)
+
+    started = []
+
+    def begin(copy):
+        copy.start()
+        started.append(copy)
+        return copy
+
+    pair_gain_copy = begin(remote(gain_ref.at[1 - side], pair_gain, pair_gain_sems, (0,), partner))
+    pair_copies = [
+        begin(remote(state_ref.at[1 - side, chunk], from_pair.at[chunk], pair_sems, (chunk,), partner))
+        for chunk in range(chunks)
+    ]
+    pair_gain_copy.wait_recv()
+    block_gain[...] = gain_ref[side] * pair_gain[...]
+    block_gains[place] = block_gain[place]
+    block_gain_copies = [
+        begin(remote(block_gain.at[other], block_gains.at[place], block_gain_sems, (step,), device))
+        for step, (other, device) in enumerate(zip(near, line))
+    ]
+    block_copies, total_copies, enter_copies, back_copies = {}, {}, {}, {}
+    section_gain_copies = []
+
+    def pair_order(chunk, slot):
+        own = state_ref[side, chunk, slot].astype(jnp.float32)
+        other = from_pair[chunk, slot].astype(jnp.float32)
+        return own, other
+
+    def stage_block(chunk):
+        pair_copies[chunk].wait_recv()
+        for slot in range(places):
+            own, other = pair_order(chunk, slot)
+            early, late = jnp.where(first, own, other), jnp.where(first, other, own)
+            late_gain = jnp.where(first, pair_gain[slot, chunk], gain_ref[side, slot, chunk])
+            block_send[chunk, slot] = (late_gain * early + late).astype(jnp.bfloat16)
+        block_recv[chunk, place] = block_send[chunk, place]
+        block_copies[chunk] = [
+            begin(remote(block_send.at[chunk, other], block_recv.at[chunk, place], block_sems, (chunk, step), device))
+            for step, (other, device) in enumerate(zip(near, line))
+        ]
+
+    def stage_total(chunk):
+        if chunk == 0:
+            for copy in block_gain_copies:
+                copy.wait_recv()
+            product = block_gains[0]
+            for slot in range(1, places):
+                product = product * block_gains[slot]
+            section_gain[...] = product
+            section_gains[section] = product
+            for step, device in enumerate(above):
+                section_gain_copies.append(
+                    begin(remote(section_gain, section_gains.at[section], section_gain_sems, (step,), device))
+                )
+        for copy in block_copies[chunk]:
+            copy.wait_recv()
+        total = block_recv[chunk, 0].astype(jnp.float32)
+        for slot in range(1, places):
+            total = block_gains[slot, chunk] * total + block_recv[chunk, slot].astype(jnp.float32)
+        total = total.astype(jnp.bfloat16)
+        total_send[chunk] = total
+        total_recv[chunk, section] = total
+        total_copies[chunk] = [
+            begin(remote(total_send.at[chunk], total_recv.at[chunk, section], total_sems, (chunk, step), device))
+            for step, device in enumerate(above)
+        ]
+
+    def stage_enter(chunk):
+        if chunk == 0:
+            for copy in section_gain_copies:
+                copy.wait_recv()
+        for copy in total_copies[chunk]:
+            copy.wait_recv()
+        now = jnp.zeros((rows, width), jnp.float32)
+        for other in range(sections - 1):
+            later = section_gains[other, chunk] * now + total_recv[chunk, other].astype(jnp.float32)
+            now = jnp.where(other < section, later, now)
+        for slot in range(places):
+            enter_send[chunk, slot] = now.astype(jnp.bfloat16)
+            if slot < places - 1:
+                now = block_gains[slot, chunk] * now + block_recv[chunk, slot].astype(jnp.float32)
+        enter_recv[chunk, place] = enter_send[chunk, place]
+        enter_copies[chunk] = [
+            begin(remote(enter_send.at[chunk, other], enter_recv.at[chunk, place], enter_sems, (chunk, step), device))
+            for step, (other, device) in enumerate(zip(near, line))
+        ]
+
+    def stage_back(chunk):
+        for copy in enter_copies[chunk]:
+            copy.wait_recv()
+        for slot in range(places):
+            own, other = pair_order(chunk, slot)
+            early = jnp.where(first, own, other)
+            early_gain = jnp.where(first, gain_ref[side, slot, chunk], pair_gain[slot, chunk])
+            into_block = enter_recv[chunk, slot]
+            into_late = (early_gain * into_block.astype(jnp.float32) + early).astype(jnp.bfloat16)
+            out_ref[side, chunk, slot] = jnp.where(first, into_block, into_late)
+            back_send[chunk, slot] = jnp.where(first, into_late, into_block)
+        back_copies[chunk] = begin(
+            remote(back_send.at[chunk], out_ref.at[side, chunk], back_sems, (chunk,), partner)
+        )
+
+    for turn in range(chunks + 3):
+        for stage, lag in ((stage_block, 0), (stage_total, 1), (stage_enter, 2), (stage_back, 3)):
+            if 0 <= turn - lag < chunks:
+                stage(turn - lag)
+    for chunk in range(chunks):
+        back_copies[chunk].wait_recv()
+    for copy in started:
+        copy.wait_send()
 
 
 def finish_kernel(within_ref, c_ref, run_ref, enter_ref, out_ref):
-    pieces = enter_ref.shape[0]
-    enter = jnp.concatenate([enter_ref[piece] for piece in range(pieces)], 1) if pieces > 1 else enter_ref[0]
+    _, chunks, places, _, _ = enter_ref.shape
+    enter = jnp.concatenate(
+        [enter_ref[0, chunk, place] for place in range(places) for chunk in range(chunks)], 1
+    )
     carried = jnp.dot(c_ref[...], enter, preferred_element_type=jnp.float32)
     gain = jnp.exp(run_ref[0])
     for pair in range(GROUP_HEADS // 2):
@@ -123,13 +254,13 @@
 
 def per_device(projected, conv_weight, conv_bias, step_size, log_decay, skip_gain):
     sections = lax.axis_size("sec")
-    targets = lax.axis_size("cp")
-    section = lax.axis_index("sec")
-    position = lax.axis_index("cp")
+    places = lax.axis_size("cp") // 2
     rows = projected.shape[0]
-    width = WIDTH_X // targets
-    pieces = GROUP_COLS // width
-    heads_here = HEAD_COUNT // targets
+    place_cols = WIDTH_X // 2 // places
+    chunks = max(1, min(CHUNKS, place_cols // 128))
+    width = place_cols // chunks
+    group_places = GROUP_COLS // place_cols
+    half_groups = G // 2
     rim = passed_along(projected[rows - RIM :], ("sec", "cp"), 1)
     lower = jnp.tril(jnp.ones((rows, rows), jnp.bfloat16))
     running = jnp.dot(lower, log_decay, preferred_element_type=jnp.float32)
@@ -140,16 +271,7 @@
     step_cols = steps_f.reshape(rows, G, GROUP_HEADS).transpose(1, 0, 2)
     skip_cols = jnp.repeat(skip_gain, P_SIZE)[None]
     bias = conv_bias[None]
-    ends = lax.all_gather(running[rows - 1 :], ("sec", "cp"), axis=0, tiled=True)
-    ends = ends.reshape(sections, targets, HEAD_COUNT)
-    ends = lax.dynamic_slice_in_dim(ends, position * heads_here, heads_here, 2)
-    mine = lax.dynamic_slice_in_dim(ends, section, 1, 0)[0]
-    gain = jnp.repeat(jnp.exp(mine), P_SIZE, axis=1)
-    through = jnp.cumsum(jnp.sum(ends, 1), axis=0)
-    before = jnp.where(section > 0, lax.dynamic_slice_in_dim(through, jnp.maximum(section - 1, 0), 1, 0), 0.0)
-    earlier = lax.broadcasted_iota(jnp.int32, through.shape, 0) < section
-    coef = jnp.where(earlier, jnp.exp(jnp.minimum(before - through, 0.0)), 0.0)
-    coef = jnp.repeat(coef, P_SIZE, axis=1)
+    gain = jnp.repeat(jnp.exp(running[rows - 1]), P_SIZE).reshape(2, places, chunks, 1, width)
 
     def spec(height, cols, first):
         return pl.BlockSpec((height, cols), lambda g: (0, first + g))
@@ -159,7 +281,10 @@
 
     group_cols = pl.BlockSpec((1, rows, GROUP_HEADS), lambda g: (g, 0, 0))
     group_rows = pl.BlockSpec((GROUP_HEADS, rows), lambda g: (g, 0))
-    piece_spec = pl.BlockSpec((pieces, N, width), lambda g: (g, 0, 0))
+    piece_spec = pl.BlockSpec(
+        (1, chunks, group_places, N, width), lambda g: (g // half_groups, 0, g % half_groups, 0, 0)
+    )
+    state_shape = jax.ShapeDtypeStruct((2, chunks, places, N, width), jnp.bfloat16)
     x, b, c, state = pl.pallas_call(
         conv_state_kernel,
         grid=(G,),
@@ -169,12 +294,11 @@
             jax.ShapeDtypeStruct((rows, WIDTH_X), jnp.bfloat16),
             jax.ShapeDtypeStruct((rows, G * N), jnp.bfloat16),
             jax.ShapeDtypeStruct((rows, G * N), jnp.bfloat16),
-            jax.ShapeDtypeStruct((targets, N, width), jnp.bfloat16),
+            state_shape,
         ],
         compiler_params=params(),
         name="conv_state",
     )(*([projected] * 3), *([rim] * 3), *([conv_weight] * 3), *([bias] * 3), run_cols, step_cols)
-    state = lax.all_to_all(state, "cp", split_axis=0, concat_axis=0, tiled=True)
     within = pl.pallas_call(
         within_kernel,
         grid=(G,),
@@ -185,20 +309,50 @@
         cost_estimate=pl.CostEstimate(flops=2 * 2 * HEAD_COUNT * rows * rows * N, bytes_accessed=8 * 1024 * 1024, transcendentals=HEAD_COUNT * rows * rows),
         name="within",
     )(x, b, c, run_cols, run_row, step_row, skip_cols)
-    total = pl.pallas_call(
-        total_kernel,
-        out_shape=jax.ShapeDtypeStruct((N, width), jnp.float32),
-        compiler_params=params(),
-        name="section_total",
+    whole = pl.BlockSpec(memory_space=pltpu.VMEM)
+
+    def held(*shape):
+        return pltpu.VMEM((*shape, N, width), jnp.bfloat16)
+
+    def gains(*shape):
+        return pltpu.VMEM((*shape, chunks, 1, width), jnp.float32)
+
+    def sems(*shape):
+        return pltpu.SemaphoreType.DMA((2, *shape))
+
+    entering = pl.pallas_call(
+        scan_kernel,
+        in_specs=[whole, whole],
+        out_specs=whole,
+        out_shape=state_shape,
+        scratch_shapes=[
+            held(chunks, places),
+            held(chunks, places),
+            held(chunks, places),
+            held(chunks),
+            held(chunks, sections),
+            held(chunks, places),
+            held(chunks, places),
+            held(chunks, places),
+            gains(places),
+            gains(places),
+            gains(places),
+            gains(),
+            gains(sections),
+            sems(chunks),
+            sems(chunks, places - 1),
+            sems(chunks, sections - 1),
+            sems(chunks, places - 1),
+            sems(chunks),
+            sems(1),
+            sems(places - 1),
+            sems(sections - 1),
+        ],
+        compiler_params=pltpu.CompilerParams(
+            vmem_limit_bytes=VMEM_LIMIT, collective_id=0, has_side_effects=True
+        ),
+        name="state_scan",
     )(state, gain)
-    totals = lax.all_gather(total, "sec", axis=0)
-    entering = pl.pallas_call(
-        entering_kernel,
-        out_shape=jax.ShapeDtypeStruct((targets, N, width), jnp.bfloat16),
-        compiler_params=params(),
-        name="entering",
-    )(state, gain, totals, coef)
-    entering = lax.all_to_all(entering, "cp", split_axis=0, concat_axis=0, tiled=True)
     return pl.pallas_call(
         finish_kernel,
         grid=(G,),

time: 232 us -> 100 us (0.43)
  the two profiles are of different devices: /device:TPU:0 before, /device:TPU:24 now
where the time goes in v2:
time: 100 us; the launch traced here: 99.9 us
  Pallas kernels  90.1 us (90%)
  local copies, waits for them, and re-layouts  3.47 us (3%)
  starting transfers between devices  3.4 us (3%)
  waiting for transfers between devices  2.62 us (3%)
    pallas_call x1, Pallas kernels, per_device(): pl.pallas_call(scan_kernel, in_specs=[whole, whole], out_specs=whole, out...  68.1 us
    pallas_call x1, Pallas kernels, per_device(): pl.pallas_call(conv_state_kernel, grid=(G,), in_specs=three(rows) + three...  8.1 us
    pallas_call x1, Pallas kernels, per_device(): pl.pallas_call(finish_kernel, grid=(G,), in_specs=[spec(rows, GROUP_COLS,...  7.5 us
    pallas_call x1, Pallas kernels, per_device(): pl.pallas_call(within_kernel, grid=(G,), in_specs=[spec(rows, GROUP_COLS,...  6.42 us
    ppermute x1, starting transfers between devices, passed_along(): lax.ppermute(value, axis, [(source, source + steps) for source in range(c...  3.4 us
    ppermute x1, waiting for transfers between devices, passed_along(): lax.ppermute(value, axis, [(source, source + steps) for source in range(c...  2.62 us
  transfers between devices with their start and end apart: 1, of which 1 were waited for; matrix products, arithmetic and copies ran while one was open for 3% of the time, Pallas kernels for 0%

profile of v2, /device:TPU:24, one launch (start us, length us, event | category | flops | bytes accessed | tf_op | source)
XLA Modules:
  0.0 99.9 jit_solution(13556396068873764669)
XLA Ops:
  0.0 0.0 copy-start
  0.0 0.0 copy-start.2
  0.0 0.0 copy-start.1
  0.0 1.0 slice.6
  1.0 3.4 %collective-permute-start = (bf16[8,10240]{1,0:T(8,128)(2,1)S(1)}, bf16[8,10240]{1,0:T(8,128)(2,1)S(1)}, u32[]{:S(2)}, u32[]{:S(2)}) collective-permute-start(bf16[8,10240]{1,0:T(8,128)(2,1)S(1)} %slice.6), channel_id=1, source_target_pairs={{0,1},{1,2},{2,3},{3,4},{4,5},{5,6},{6,7},{7,8},{8,9},{9,10},{10,1... | collective-permute-start | bytes 491528 | tf_op jit(solution)/shard_map/ppermute | solution.py:24
  4.4 0.0 copy-done
  4.4 0.1 fusion.1
  4.6 0.1 copy.10
  4.7 0.9 copy.12
  5.5 0.1 exp.8
  5.7 0.1 broadcast_in_dim.22
  5.8 0.1 broadcast_in_dim.23.gain_ref
  5.9 0.7 broadcast_in_dim.21
  6.6 0.1 broadcast_in_dim_reshape.3.skip_ref
  6.7 0.2 copy.11
  6.9 0.1 copy.13
  7.1 2.6 %collective-permute-done.rx.rb.rc = bf16[8,10240]{1,0:T(8,128)(2,1)S(1)} collective-permute-done((bf16[8,10240]{1,0:T(8,128)(2,1)S(1)}, bf16[8,10240]{1,0:T(8,128)(2,1)S(1)}, u32[]{:S(2)}, u32[]{:S(2)}) %collective-permute-start) | collective-permute-done | bytes 163872 | tf_op jit(solution)/shard_map/ppermute | solution.py:24
  9.7 0.0 copy-done.2
  9.7 0.0 copy-done.1
  9.7 8.1 %conv_state.1 = (bf16[128,8192]{1,0:T(8,128)(2,1)S(1)}, bf16[128,1024]{1,0:T(8,128)(2,1)S(1)}, bf16[128,1024]{1,0:T(8,128)(2,1)S(1)}, bf16[2,4,4,128,256]{4,3,2,1,0:T(8,128)(2,1)S(1)}) custom-call(bf16[128,10240]{1,0:T(8,128)(2,1)} %pc.1, bf16[128,10240]{1,0:T(8,128)(2,1)} %pc.1, bf16[128,10240]{1,0:T(8,128)(2,1)} %pc.1, ...), custom_call_target="tpu_custom_call" | custom-call | tf_op jit(solution)/shard_map/conv_state/pallas_call | solution.py:288
  17.8 68.1 %state_scan.1.enter_ref = bf16[2,4,4,128,256]{4,3,2,1,0:T(8,128)(2,1)S(1)} custom-call(bf16[2,4,4,128,256]{4,3,2,1,0:T(8,128)(2,1)S(1)} %get-tuple-element.12.state_ref, f32[2,4,4,1,256]{4,3,2,1,0:T(1,128)S(1)} %broadcast_in_dim.23.gain_ref), custom_call_target="tpu_custom_call" | custom-call | tf_op jit(solution)/shard_map/state_scan/pallas_call | solution.py:323
  85.9 6.4 %within.1.within_ref = f32[128,8192]{1,0:T(8,128)} custom-call(bf16[128,8192]{1,0:T(8,128)(2,1)S(1)} %get-tuple-element.9.x_ref, bf16[128,1024]{1,0:T(8,128)(2,1)S(1)} %get-tuple-element.10.b_ref, bf16[128,1024]{1,0:T(8,128)(2,1)S(1)} %get-tuple-element.11.c_ref, f32[8,128,16]{2,1,0:T(8,128)S(1)} %bitcast.11, f32[128,128]{1,0:T(8,128)S(1)} %bitcast.15, ...), custom_call_target="tpu_custom_call" | custom-call | flops 1073741824 | bytes 8388608 | tf_op jit(solution)/shard_map/within/pallas_call | solution.py:302
  92.4 7.5 %finish.1 = bf16[128,8192]{1,0:T(8,128)(2,1)} custom-call(f32[128,8192]{1,0:T(8,128)} %within.1.within_ref, bf16[128,1024]{1,0:T(8,128)(2,1)S(1)} %get-tuple-element.11.c_ref, f32[8,128,16]{2,1,0:T(8,128)S(1)} %bitcast.12, bf16[2,4,4,128,256]{4,3,2,1,0:T(8,128)(2,1)S(1)} %state_scan.1.enter_ref), custom_call_target="tpu_custom_call" | custom-call | tf_op jit(solution)/shard_map/finish/pallas_call | solution.py:356
  (2 shorter events, 0.0 us)
Async XLA Ops:
  0.0 4.4 %copy-start = (bf16[128,128]{1,0:T(8,128)(2,1)S(1)}, bf16[128,128]{1,0:T(8,128)(2,1)}, u32[]{:S(2)}) copy-start(bf16[128,128]{1,0:T(8,128)(2,1)} %param.10) | copy-start | bytes 98308
  0.0 9.7 %copy-start.2 = (f32[10240]{0:T(1024)S(1)}, f32[10240]{0:T(1024)}, u32[]{:S(2)}) copy-start(f32[10240]{0:T(1024)} %param.8) | copy-start | bytes 122884
  0.0 9.7 %copy-start.1 = (f32[4,10240]{1,0:T(4,128)S(1)}, f32[4,10240]{1,0:T(4,128)}, u32[]{:S(2)}) copy-start(f32[4,10240]{1,0:T(4,128)} %wc.1) | copy-start | bytes 491524
  1.0 8.7 %collective-permute-start = (bf16[8,10240]{1,0:T(8,128)(2,1)S(1)}, bf16[8,10240]{1,0:T(8,128)(2,1)S(1)}, u32[]{:S(2)}, u32[]{:S(2)}) collective-permute-start(bf16[8,10240]{1,0:T(8,128)(2,1)S(1)} %slice.6), channel_id=1, source_target_pairs={{0,1},{1,2},{2,3},{3,4},{4,5},{5,6},{6,7},{7,8},{8,9},{9,10},{10,1... | collective-permute-start | bytes 491528 | tf_op jit(solution)/shard_map/ppermute | solution.py:24

commit v3 on v2

--- a/solution.py
+++ b/solution.py
@@ -15,7 +15,6 @@
 GROUP_COLS = GROUP_HEADS * P_SIZE
 WIDTH_X = HEAD_COUNT * P_SIZE
 RIM = 8
-CHUNKS = 4
 VMEM_LIMIT = 48 * 1024 * 1024
 
 
@@ -69,32 +68,9 @@
             state_out[0, chunk, place] = state[:, begin : begin + width]
 
 
-def within_kernel(x_ref, b_ref, c_ref, run_ref, run_row_ref, step_row_ref, skip_ref, out_ref):
-    rows = x_ref.shape[0]
-    scores = lax.dot_general(
-        c_ref[...], b_ref[...], (((1,), (1,)), ((), ())), preferred_element_type=jnp.float32
-    )
-    token = lax.broadcasted_iota(jnp.int32, (rows, rows), 0)
-    source = lax.broadcasted_iota(jnp.int32, (rows, rows), 1)
-    scores = jnp.where(token >= source, scores, 0.0)
-    run = run_ref[0]
-    lane = lax.broadcasted_iota(jnp.int32, (rows, 2 * P_SIZE), 1)
-    for pair in range(GROUP_HEADS // 2):
-        columns = slice(pair * 2 * P_SIZE, (pair + 1) * 2 * P_SIZE)
-        x = x_ref[:, columns]
-        found = []
-        for head in (2 * pair, 2 * pair + 1):
-            gap = run[:, head : head + 1] - run_row_ref[head : head + 1, :]
-            mix = scores * jnp.exp(jnp.minimum(gap, 0.0)) * step_row_ref[head : head + 1, :]
-            found.append(jnp.dot(mix.astype(jnp.bfloat16), x, preferred_element_type=jnp.float32))
-        out_ref[:, columns] = (
-            jnp.where(lane < P_SIZE, found[0], found[1]) + skip_ref[:, columns] * x.astype(jnp.float32)
-        )
-
-
 def scan_kernel(
-    state_ref, gain_ref, out_ref,
-    from_pair, block_send, block_recv, total_send, total_recv, enter_send, enter_recv, back_send,
+    state_ref, gain_ref, x_ref, b_ref, c_ref, run_ref, run_row_ref, step_row_ref, skip_ref, out_ref,
+    enter_ref, run_pair, scores_ref, within_ref, from_pair, block_send, block_recv, total_send, total_recv, enter_send, enter_recv, back_send,
     pair_gain, block_gain, block_gains, section_gain, section_gains,
     pair_sems, block_sems, total_sems, enter_sems, back_sems, pair_gain_sems, block_gain_sems, section_gain_sems,
 ):
@@ -102,6 +78,8 @@
     section, position = lax.axis_index("sec"), lax.axis_index("cp")
     place, side = position // 2, position % 2
     _, chunks, places, rows, width = state_ref.shape
+    tokens = x_ref.shape[0]
+    lane = lax.broadcasted_iota(jnp.int32, (tokens, width), 1)
     first = side == 0
     partner = (section, place * 2 + (1 - side))
     near = [lax.rem(place + step, places) for step in range(1, places)]
@@ -135,6 +113,64 @@
         begin(remote(state_ref.at[1 - side, chunk], from_pair.at[chunk], pair_sems, (chunk,), partner))
         for chunk in range(chunks)
     ]
+
+    for pair in range(HEAD_COUNT // 2):
+        run_pair[pair] = run_ref[:, 2 * pair : 2 * pair + 2]
+    token = lax.broadcasted_iota(jnp.int32, (tokens, tokens), 0)
+    causal = token >= lax.broadcasted_iota(jnp.int32, (tokens, tokens), 1)
+
+    def group_scores(group, carry):
+        columns = pl.ds(pl.multiple_of(group * N, N), N)
+        scores = lax.dot_general(
+            c_ref[:, columns], b_ref[:, columns], (((1,), (1,)), ((), ())), preferred_element_type=jnp.float32
+        )
+        scores_ref[group] = jnp.where(causal, scores, 0.0)
+        return carry
+
+    lax.fori_loop(0, G, group_scores, 0)
+
+    def stage_within(chunk):
+        def one_place(slot, carry):
+            for half in range(2):
+                pair = (half * places + slot) * chunks + chunk
+                columns = pl.ds(pl.multiple_of(pair * width, width), width)
+                scores = scores_ref[lax.div(pair, GROUP_HEADS // 2)]
+                x = x_ref[:, columns]
+                run = run_pair[pair]
+                run_row = run_row_ref[pair]
+                step_row = step_row_ref[pair]
+                found = []
+                for head in range(2):
+                    gap = run[:, head : head + 1] - run_row[head : head + 1, :]
+                    mix = scores * jnp.exp(jnp.minimum(gap, 0.0)) * step_row[head : head + 1, :]
+                    found.append(jnp.dot(mix.astype(jnp.bfloat16), x, preferred_element_type=jnp.float32))
+                within_ref[pair] = (
+                    jnp.where(lane < P_SIZE, found[0], found[1]) + skip_ref[pair] * x.astype(jnp.float32)
+                )
+            return carry
+
+        lax.fori_loop(0, places, one_place, 0)
+
+    def stage_finish(chunk):
+        back_copies[chunk].wait_recv()
+
+        def one_place(slot, carry):
+            for half in range(2):
+                pair = (half * places + slot) * chunks + chunk
+                group = lax.div(pair, GROUP_HEADS // 2)
+                carried = jnp.dot(
+                    c_ref[:, pl.ds(pl.multiple_of(group * N, N), N)],
+                    enter_ref[half, chunk, slot],
+                    preferred_element_type=jnp.float32,
+                )
+                gain = jnp.exp(run_pair[pair])
+                out_ref[:, pl.ds(pl.multiple_of(pair * width, width), width)] = (
+                    within_ref[pair] + spread(gain, 0) * carried
+                ).astype(jnp.bfloat16)
+            return carry
+
+        lax.fori_loop(0, places, one_place, 0)
+
     pair_gain_copy.wait_recv()
     block_gain[...] = gain_ref[side] * pair_gain[...]
     block_gains[place] = block_gain[place]
@@ -218,34 +254,19 @@
             early_gain = jnp.where(first, gain_ref[side, slot, chunk], pair_gain[slot, chunk])
             into_block = enter_recv[chunk, slot]
             into_late = (early_gain * into_block.astype(jnp.float32) + early).astype(jnp.bfloat16)
-            out_ref[side, chunk, slot] = jnp.where(first, into_block, into_late)
+            enter_ref[side, chunk, slot] = jnp.where(first, into_block, into_late)
             back_send[chunk, slot] = jnp.where(first, into_late, into_block)
         back_copies[chunk] = begin(
-            remote(back_send.at[chunk], out_ref.at[side, chunk], back_sems, (chunk,), partner)
+            remote(back_send.at[chunk], enter_ref.at[side, chunk], back_sems, (chunk,), partner)
         )
 
-    for turn in range(chunks + 3):
-        for stage, lag in ((stage_block, 0), (stage_total, 1), (stage_enter, 2), (stage_back, 3)):
+    plan = ((stage_block, 0), (stage_within, 0), (stage_total, 1), (stage_enter, 2), (stage_back, 3), (stage_finish, 4))
+    for turn in range(chunks + 4):
+        for stage, lag in plan:
             if 0 <= turn - lag < chunks:
                 stage(turn - lag)
-    for chunk in range(chunks):
-        back_copies[chunk].wait_recv()
     for copy in started:
         copy.wait_send()
-
-
-def finish_kernel(within_ref, c_ref, run_ref, enter_ref, out_ref):
-    _, chunks, places, _, _ = enter_ref.shape
-    enter = jnp.concatenate(
-        [enter_ref[0, chunk, place] for place in range(places) for chunk in range(chunks)], 1
-    )
-    carried = jnp.dot(c_ref[...], enter, preferred_element_type=jnp.float32)
-    gain = jnp.exp(run_ref[0])
-    for pair in range(GROUP_HEADS // 2):
-        columns = slice(pair * 2 * P_SIZE, (pair + 1) * 2 * P_SIZE)
-        out_ref[:, columns] = (
-            within_ref[:, columns] + spread(gain, pair) * carried[:, columns]
-        ).astype(jnp.bfloat16)
 
 
 def params():
@@ -257,19 +278,20 @@
     places = lax.axis_size("cp") // 2
     rows = projected.shape[0]
     place_cols = WIDTH_X // 2 // places
-    chunks = max(1, min(CHUNKS, place_cols // 128))
-    width = place_cols // chunks
+    width = 2 * P_SIZE
+    chunks = place_cols // width
+    pairs = HEAD_COUNT // 2
     group_places = GROUP_COLS // place_cols
     half_groups = G // 2
     rim = passed_along(projected[rows - RIM :], ("sec", "cp"), 1)
     lower = jnp.tril(jnp.ones((rows, rows), jnp.bfloat16))
     running = jnp.dot(lower, log_decay, preferred_element_type=jnp.float32)
-    run_row = running.T
+    run_row = running.T.reshape(pairs, 2, rows)
     run_cols = running.reshape(rows, G, GROUP_HEADS).transpose(1, 0, 2)
     steps_f = step_size.astype(jnp.float32)
-    step_row = steps_f.T
+    step_row = steps_f.T.reshape(pairs, 2, rows)
     step_cols = steps_f.reshape(rows, G, GROUP_HEADS).transpose(1, 0, 2)
-    skip_cols = jnp.repeat(skip_gain, P_SIZE)[None]
+    skip_cols = jnp.repeat(skip_gain, P_SIZE).reshape(pairs, 1, width)
     bias = conv_bias[None]
     gain = jnp.repeat(jnp.exp(running[rows - 1]), P_SIZE).reshape(2, places, chunks, 1, width)
 
@@ -280,7 +302,6 @@
         return [spec(height, GROUP_COLS, 0), spec(height, N, WIDTH_X // N), spec(height, N, WIDTH_X // N + G)]
 
     group_cols = pl.BlockSpec((1, rows, GROUP_HEADS), lambda g: (g, 0, 0))
-    group_rows = pl.BlockSpec((GROUP_HEADS, rows), lambda g: (g, 0))
     piece_spec = pl.BlockSpec(
         (1, chunks, group_places, N, width), lambda g: (g // half_groups, 0, g % half_groups, 0, 0)
     )
@@ -299,16 +320,6 @@
         compiler_params=params(),
         name="conv_state",
     )(*([projected] * 3), *([rim] * 3), *([conv_weight] * 3), *([bias] * 3), run_cols, step_cols)
-    within = pl.pallas_call(
-        within_kernel,
-        grid=(G,),
-        in_specs=[spec(rows, GROUP_COLS, 0), spec(rows, N, 0), spec(rows, N, 0), group_cols, group_rows, group_rows, spec(1, GROUP_COLS, 0)],
-        out_specs=spec(rows, GROUP_COLS, 0),
-        out_shape=jax.ShapeDtypeStruct((rows, WIDTH_X), jnp.float32),
-        compiler_params=params(),
-        cost_estimate=pl.CostEstimate(flops=2 * 2 * HEAD_COUNT * rows * rows * N, bytes_accessed=8 * 1024 * 1024, transcendentals=HEAD_COUNT * rows * rows),
-        name="within",
-    )(x, b, c, run_cols, run_row, step_row, skip_cols)
     whole = pl.BlockSpec(memory_space=pltpu.VMEM)
 
     def held(*shape):
@@ -320,12 +331,16 @@
     def sems(*shape):
         return pltpu.SemaphoreType.DMA((2, *shape))
 
-    entering = pl.pallas_call(
+    return pl.pallas_call(
         scan_kernel,
-        in_specs=[whole, whole],
+        in_specs=[whole] * 9,
         out_specs=whole,
-        out_shape=state_shape,
+        out_shape=jax.ShapeDtypeStruct((rows, WIDTH_X), jnp.bfloat16),
         scratch_shapes=[
+            held(2, chunks, places),
+            pltpu.VMEM((pairs, rows, 2), jnp.float32),
+            pltpu.VMEM((G, rows, rows), jnp.float32),
+            pltpu.VMEM((pairs, rows, width), jnp.float32),
             held(chunks, places),
             held(chunks, places),
             held(chunks, places),
@@ -352,16 +367,7 @@
             vmem_limit_bytes=VMEM_LIMIT, collective_id=0, has_side_effects=True
         ),
         name="state_scan",
-    )(state, gain)
-    return pl.pallas_call(
-        finish_kernel,
-        grid=(G,),
-        in_specs=[spec(rows, GROUP_COLS, 0), spec(rows, N, 0), group_cols, piece_spec],
-        out_specs=spec(rows, GROUP_COLS, 0),
-        out_shape=jax.ShapeDtypeStruct((rows, WIDTH_X), jnp.bfloat16),
-        compiler_params=params(),
-        name="finish",
-    )(within, c, run_cols, entering)
+    )(state, gain, x, b, c, running, run_row, step_row, skip_cols)
 
 
 def solution(mesh):

time: 100 us -> 89.1 us (0.89)
  the two profiles are of different devices: /device:TPU:24 before, /device:TPU:0 now
where the time goes in v3:
time: 89.1 us; the launch traced here: 88.7 us
  Pallas kernels  76.7 us (86%)
  local copies, waits for them, and re-layouts  6.55 us (7%)
  starting transfers between devices  4.86 us (5%)
    pallas_call x1, Pallas kernels, per_device(): pl.pallas_call(scan_kernel, in_specs=[whole] * 9, out_specs=whole, out_sh...  68.7 us
    pallas_call x1, Pallas kernels, per_device(): pl.pallas_call(conv_state_kernel, grid=(G,), in_specs=three(rows) + three...  8.1 us
    ppermute x1, starting transfers between devices, passed_along(): lax.ppermute(value, axis, [(source, source + steps) for source in range(c...  4.86 us
    unnamed x10, local copies, waits for them, and re-layouts  3.52 us
  transfers between devices with their start and end apart: 1, of which 1 were waited for; matrix products, arithmetic and copies ran while one was open for 4% of the time, Pallas kernels for 0%

profile of v3, /device:TPU:0, one launch (start us, length us, event | category | flops | bytes accessed | tf_op | source)
XLA Modules:
  0.0 88.7 jit_solution(8274738318181313247)
XLA Ops:
  0.0 0.0 copy-start
  0.0 0.0 copy-start.3
  0.0 0.0 copy-start.2
  0.0 1.0 %slice.6 = bf16[8,10240]{1,0:T(8,128)(2,1)S(1)} slice(bf16[128,10240]{1,0:T(8,128)(2,1)} %pc.1), slice={[120:128], [0:10240]} | slice | bytes 327680 | tf_op jit(solution)/shard_map/slice | solution.py:286
  1.0 4.9 %collective-permute-start = (bf16[8,10240]{1,0:T(8,128)(2,1)S(1)}, bf16[8,10240]{1,0:T(8,128)(2,1)S(1)}, u32[]{:S(2)}, u32[]{:S(2)}) collective-permute-start(bf16[8,10240]{1,0:T(8,128)(2,1)S(1)} %slice.6), channel_id=1, source_target_pairs={{0,1},{1,2},{2,3},{3,4},{4,5},{5,6},{6,7},{7,8},{8,9},{9,10},{10,1... | collective-permute-start | bytes 491528 | tf_op jit(solution)/shard_map/ppermute | solution.py:23
  5.8 0.0 copy-done
  5.9 0.2 fusion.2
  6.1 0.9 copy.10
  7.0 0.8 broadcast_in_dim.27
  7.7 0.1 broadcast_in_dim.28
  7.9 0.1 broadcast_in_dim.29.skip_ref
  8.0 0.1 copy.12.run_ref
  8.1 0.2 fusion
  8.3 0.1 exp.8
  8.4 0.1 broadcast_in_dim.25
  8.6 0.1 broadcast_in_dim.26.gain_ref
  8.7 0.2 copy.9
  8.9 0.2 copy.11
  9.1 0.2 collective-permute-done.rx.rb.rc
  9.3 0.0 copy-done.3
  9.3 0.0 copy-done.2
  9.3 8.1 %conv_state.1 = (bf16[128,8192]{1,0:T(8,128)(2,1)S(1)}, bf16[128,1024]{1,0:T(8,128)(2,1)S(1)}, bf16[128,1024]{1,0:T(8,128)(2,1)S(1)}, bf16[2,8,4,128,128]{4,3,2,1,0:T(8,128)(2,1)S(1)}) custom-call(bf16[128,10240]{1,0:T(8,128)(2,1)} %pc.1, bf16[128,10240]{1,0:T(8,128)(2,1)} %pc.1, bf16[128,10240]{1,0:T(8,128)(2,1)} %pc.1, ...), custom_call_target="tpu_custom_call" | custom-call | tf_op jit(solution)/shard_map/conv_state/pallas_call | solution.py:309
  17.4 0.0 copy-start.1
  17.4 1.3 %copy-done.1 = bf16[128,8192]{1,0:T(8,128)(2,1)} copy-done((bf16[128,8192]{1,0:T(8,128)(2,1)}, bf16[128,8192]{1,0:T(8,128)(2,1)S(1)}, u32[]{:S(2)}) %copy-start.1) | copy-done | bytes 2097176
  18.7 68.7 %state_scan.1 = bf16[128,8192]{1,0:T(8,128)(2,1)S(1)} custom-call(bf16[2,8,4,128,128]{4,3,2,1,0:T(8,128)(2,1)S(1)} %get-tuple-element.9.state_ref, f32[2,4,8,1,128]{4,3,2,1,0:T(1,128)S(1)} %broadcast_in_dim.26.gain_ref, bf16[128,8192]{1,0:T(8,128)(2,1)} %copy-done.1, bf16[128,1024]{1,0:T(8,128)(2,1)S(1)} %get-tuple-element.11.b_ref, ...), custom_call_target="tpu_custom_call" | custom-call | tf_op jit(solution)/shard_map/state_scan/pallas_call | solution.py:334
  87.4 1.3 %copy.14 = bf16[128,8192]{1,0:T(8,128)(2,1)} copy(bf16[128,8192]{1,0:T(8,128)(2,1)S(1)} %state_scan.1) | data formatting | bytes 4194304
  (1 shorter events, 0.0 us)
Async XLA Ops:
  0.0 5.8 %copy-start = (bf16[128,128]{1,0:T(8,128)(2,1)S(1)}, bf16[128,128]{1,0:T(8,128)(2,1)}, u32[]{:S(2)}) copy-start(bf16[128,128]{1,0:T(8,128)(2,1)} %param.10) | copy-start | bytes 98308
  0.0 9.3 %copy-start.3 = (f32[10240]{0:T(1024)S(1)}, f32[10240]{0:T(1024)}, u32[]{:S(2)}) copy-start(f32[10240]{0:T(1024)} %param.8) | copy-start | bytes 122884
  0.0 9.3 %copy-start.2 = (f32[4,10240]{1,0:T(4,128)S(1)}, f32[4,10240]{1,0:T(4,128)}, u32[]{:S(2)}) copy-start(f32[4,10240]{1,0:T(4,128)} %wc.1) | copy-start | bytes 491524
  1.0 8.3 %collective-permute-start = (bf16[8,10240]{1,0:T(8,128)(2,1)S(1)}, bf16[8,10240]{1,0:T(8,128)(2,1)S(1)}, u32[]{:S(2)}, u32[]{:S(2)}) collective-permute-start(bf16[8,10240]{1,0:T(8,128)(2,1)S(1)} %slice.6), channel_id=1, source_target_pairs={{0,1},{1,2},{2,3},{3,4},{4,5},{5,6},{6,7},{7,8},{8,9},{9,10},{10,1... | collective-permute-start | bytes 491528 | tf_op jit(solution)/shard_map/ppermute | solution.py:23
  17.4 1.3 %copy-start.1 = (bf16[128,8192]{1,0:T(8,128)(2,1)}, bf16[128,8192]{1,0:T(8,128)(2,1)S(1)}, u32[]{:S(2)}) copy-start(bf16[128,8192]{1,0:T(8,128)(2,1)S(1)} %get-tuple-element.10.x_ref) | copy-start | bytes 6291460

commit v4 on v3

--- a/solution.py
+++ b/solution.py
@@ -15,6 +15,7 @@
 GROUP_COLS = GROUP_HEADS * P_SIZE
 WIDTH_X = HEAD_COUNT * P_SIZE
 RIM = 8
+IN_FLIGHT = 3
 VMEM_LIMIT = 48 * 1024 * 1024
 
 
@@ -33,7 +34,8 @@
         top = jnp.where(row < back, pltpu.roll(rim, back, 0), moved[:RIM])
         moved = jnp.concatenate([top, moved[RIM:]], 0)
         total = total + weight_ref[KERNEL - 1 - back : KERNEL - back, :] * moved
-    return (total / (1.0 + jnp.exp(-total))).astype(jnp.bfloat16)
+    half = 0.5 * total
+    return (half * jnp.tanh(half) + half).astype(jnp.bfloat16)
 
 
 def spread(columns, pair):
@@ -109,10 +111,17 @@
         return copy
 
     pair_gain_copy = begin(remote(gain_ref.at[1 - side], pair_gain, pair_gain_sems, (0,), partner))
-    pair_copies = [
-        begin(remote(state_ref.at[1 - side, chunk], from_pair.at[chunk], pair_sems, (chunk,), partner))
-        for chunk in range(chunks)
-    ]
+    pair_copies = []
+
+    def send_pair():
+        chunk = len(pair_copies)
+        if chunk < chunks:
+            pair_copies.append(
+                begin(remote(state_ref.at[1 - side, chunk], from_pair.at[chunk], pair_sems, (chunk,), partner))
+            )
+
+    for _ in range(IN_FLIGHT):
+        send_pair()
 
     for pair in range(HEAD_COUNT // 2):
         run_pair[pair] = run_ref[:, 2 * pair : 2 * pair + 2]
@@ -188,6 +197,7 @@
 
     def stage_block(chunk):
         pair_copies[chunk].wait_recv()
+        send_pair()
         for slot in range(places):
             own, other = pair_order(chunk, slot)
             early, late = jnp.where(first, own, other), jnp.where(first, other, own)
@@ -260,7 +270,8 @@
             remote(back_send.at[chunk], enter_ref.at[side, chunk], back_sems, (chunk,), partner)
         )
 
-    plan = ((stage_block, 0), (stage_within, 0), (stage_total, 1), (stage_enter, 2), (stage_back, 3), (stage_finish, 4))
+    plan = ((stage_block, 0), (stage_within, -1), (stage_total, 1), (stage_enter, 2), (stage_back, 3), (stage_finish, 4))
+    stage_within(0)
     for turn in range(chunks + 4):
         for stage, lag in plan:
             if 0 <= turn - lag < chunks:

time: 89.1 us -> 89.1 us (level)
  no operation moved by 1% of the time
where the time goes in v4:
time: 89.1 us; the launch traced here: 88.7 us
  Pallas kernels  76.7 us (86%)
  local copies, waits for them, and re-layouts  6.55 us (7%)
  starting transfers between devices  4.86 us (5%)
    pallas_call x1, Pallas kernels, per_device(): pl.pallas_call(scan_kernel, in_specs=[whole] * 9, out_specs=whole, out_sh...  68.8 us
    pallas_call x1, Pallas kernels, per_device(): pl.pallas_call(conv_state_kernel, grid=(G,), in_specs=three(rows) + three...  7.98 us
    ppermute x1, starting transfers between devices, passed_along(): lax.ppermute(value, axis, [(source, source + steps) for source in range(c...  4.86 us
    unnamed x10, local copies, waits for them, and re-layouts  3.52 us
  transfers between devices with their start and end apart: 1, of which 1 were waited for; matrix products, arithmetic and copies ran while one was open for 4% of the time, Pallas kernels for 0%

profile of v4, /device:TPU:0, one launch (start us, length us, event | category | flops | bytes accessed | tf_op | source)
XLA Modules:
  0.0 88.7 jit_solution(34165895913185159)
XLA Ops:
  0.0 0.0 copy-start
  0.0 0.0 copy-start.3
  0.0 0.0 copy-start.2
  0.0 1.0 %slice.6 = bf16[8,10240]{1,0:T(8,128)(2,1)S(1)} slice(bf16[128,10240]{1,0:T(8,128)(2,1)} %pc.1), slice={[120:128], [0:10240]} | slice | bytes 327680 | tf_op jit(solution)/shard_map/slice | solution.py:297
  1.0 4.9 %collective-permute-start = (bf16[8,10240]{1,0:T(8,128)(2,1)S(1)}, bf16[8,10240]{1,0:T(8,128)(2,1)S(1)}, u32[]{:S(2)}, u32[]{:S(2)}) collective-permute-start(bf16[8,10240]{1,0:T(8,128)(2,1)S(1)} %slice.6), channel_id=1, source_target_pairs={{0,1},{1,2},{2,3},{3,4},{4,5},{5,6},{6,7},{7,8},{8,9},{9,10},{10,1... | collective-permute-start | bytes 491528 | tf_op jit(solution)/shard_map/ppermute | solution.py:24
  5.8 0.0 copy-done
  5.9 0.2 fusion.2
  6.1 0.9 copy.10
  7.0 0.8 broadcast_in_dim.27
  7.7 0.1 broadcast_in_dim.28
  7.9 0.1 broadcast_in_dim.29.skip_ref
  8.0 0.1 copy.12.run_ref
  8.1 0.2 fusion
  8.3 0.1 exp.8
  8.4 0.1 broadcast_in_dim.25
  8.6 0.1 broadcast_in_dim.26.gain_ref
  8.7 0.2 copy.9
  8.9 0.2 copy.11
  9.1 0.2 collective-permute-done.rx.rb.rc
  9.3 0.0 copy-done.3
  9.3 0.0 copy-done.2
  9.3 8.0 %conv_state.1 = (bf16[128,8192]{1,0:T(8,128)(2,1)S(1)}, bf16[128,1024]{1,0:T(8,128)(2,1)S(1)}, bf16[128,1024]{1,0:T(8,128)(2,1)S(1)}, bf16[2,8,4,128,128]{4,3,2,1,0:T(8,128)(2,1)S(1)}) custom-call(bf16[128,10240]{1,0:T(8,128)(2,1)} %pc.1, bf16[128,10240]{1,0:T(8,128)(2,1)} %pc.1, bf16[128,10240]{1,0:T(8,128)(2,1)} %pc.1, ...), custom_call_target="tpu_custom_call" | custom-call | tf_op jit(solution)/shard_map/conv_state/pallas_call | solution.py:320
  17.3 0.0 copy-start.1
  17.3 1.3 %copy-done.1 = bf16[128,8192]{1,0:T(8,128)(2,1)} copy-done((bf16[128,8192]{1,0:T(8,128)(2,1)}, bf16[128,8192]{1,0:T(8,128)(2,1)S(1)}, u32[]{:S(2)}) %copy-start.1) | copy-done | bytes 2097176
  18.6 68.8 %state_scan.1 = bf16[128,8192]{1,0:T(8,128)(2,1)S(1)} custom-call(bf16[2,8,4,128,128]{4,3,2,1,0:T(8,128)(2,1)S(1)} %get-tuple-element.9.state_ref, f32[2,4,8,1,128]{4,3,2,1,0:T(1,128)S(1)} %broadcast_in_dim.26.gain_ref, bf16[128,8192]{1,0:T(8,128)(2,1)} %copy-done.1, bf16[128,1024]{1,0:T(8,128)(2,1)S(1)} %get-tuple-element.11.b_ref, ...), custom_call_target="tpu_custom_call" | custom-call | tf_op jit(solution)/shard_map/state_scan/pallas_call | solution.py:345
  87.4 1.3 %copy.14 = bf16[128,8192]{1,0:T(8,128)(2,1)} copy(bf16[128,8192]{1,0:T(8,128)(2,1)S(1)} %state_scan.1) | data formatting | bytes 4194304
  (1 shorter events, 0.0 us)
Async XLA Ops:
  0.0 5.8 %copy-start = (bf16[128,128]{1,0:T(8,128)(2,1)S(1)}, bf16[128,128]{1,0:T(8,128)(2,1)}, u32[]{:S(2)}) copy-start(bf16[128,128]{1,0:T(8,128)(2,1)} %param.10) | copy-start | bytes 98308
  0.0 9.3 %copy-start.3 = (f32[10240]{0:T(1024)S(1)}, f32[10240]{0:T(1024)}, u32[]{:S(2)}) copy-start(f32[10240]{0:T(1024)} %param.8) | copy-start | bytes 122884
  0.0 9.3 %copy-start.2 = (f32[4,10240]{1,0:T(4,128)S(1)}, f32[4,10240]{1,0:T(4,128)}, u32[]{:S(2)}) copy-start(f32[4,10240]{1,0:T(4,128)} %wc.1) | copy-start | bytes 491524
  1.0 8.3 %collective-permute-start = (bf16[8,10240]{1,0:T(8,128)(2,1)S(1)}, bf16[8,10240]{1,0:T(8,128)(2,1)S(1)}, u32[]{:S(2)}, u32[]{:S(2)}) collective-permute-start(bf16[8,10240]{1,0:T(8,128)(2,1)S(1)} %slice.6), channel_id=1, source_target_pairs={{0,1},{1,2},{2,3},{3,4},{4,5},{5,6},{6,7},{7,8},{8,9},{9,10},{10,1... | collective-permute-start | bytes 491528 | tf_op jit(solution)/shard_map/ppermute | solution.py:24
  17.3 1.3 %copy-start.1 = (bf16[128,8192]{1,0:T(8,128)(2,1)}, bf16[128,8192]{1,0:T(8,128)(2,1)S(1)}, u32[]{:S(2)}) copy-start(bf16[128,8192]{1,0:T(8,128)(2,1)S(1)} %get-tuple-element.10.x_ref) | copy-start | bytes 6291460

commit v5 on v3

--- a/solution.py
+++ b/solution.py
@@ -260,7 +260,7 @@
             remote(back_send.at[chunk], enter_ref.at[side, chunk], back_sems, (chunk,), partner)
         )
 
-    plan = ((stage_block, 0), (stage_within, 0), (stage_total, 1), (stage_enter, 2), (stage_back, 3), (stage_finish, 4))
+    plan = ((stage_back, 3), (stage_enter, 2), (stage_total, 1), (stage_block, 0), (stage_within, 0), (stage_finish, 4))
     for turn in range(chunks + 4):
         for stage, lag in plan:
             if 0 <= turn - lag < chunks:

time: 89.1 us -> 93.2 us (1.046)
  Pallas kernels: 76.7 us -> 80.8 us
    pallas_call x1, Pallas kernels: 68.7 us -> 72.7 us  [per_device(): pl.pallas_call(scan_kernel, in_specs=[whole] * 9, out_specs=whole, out_sh...]
  transfers between devices with their start and end apart: 1 -> 1, of which waited for: 1 -> 1; matrix products, arithmetic and copies ran while one was open for 4% -> 3% of each run, Pallas kernels for 0% -> 0%
where the time goes in v5:
time: 93.2 us; the launch traced here: 92.8 us
  Pallas kernels  80.8 us (87%)
  local copies, waits for them, and re-layouts  6.55 us (7%)
  starting transfers between devices  4.86 us (5%)
    pallas_call x1, Pallas kernels, per_device(): pl.pallas_call(scan_kernel, in_specs=[whole] * 9, out_specs=whole, out_sh...  72.7 us
    pallas_call x1, Pallas kernels, per_device(): pl.pallas_call(conv_state_kernel, grid=(G,), in_specs=three(rows) + three...  8.1 us
    ppermute x1, starting transfers between devices, passed_along(): lax.ppermute(value, axis, [(source, source + steps) for source in range(c...  4.86 us
    unnamed x10, local copies, waits for them, and re-layouts  3.52 us
  transfers between devices with their start and end apart: 1, of which 1 were waited for; matrix products, arithmetic and copies ran while one was open for 3% of the time, Pallas kernels for 0%

profile of v5, /device:TPU:0, one launch (start us, length us, event | category | flops | bytes accessed | tf_op | source)
XLA Modules:
  0.0 92.8 jit_solution(17860942446283771659)
XLA Ops:
  0.0 0.0 copy-start
  0.0 0.0 copy-start.3
  0.0 0.0 copy-start.2
  0.0 1.0 %slice.6 = bf16[8,10240]{1,0:T(8,128)(2,1)S(1)} slice(bf16[128,10240]{1,0:T(8,128)(2,1)} %pc.1), slice={[120:128], [0:10240]} | slice | bytes 327680 | tf_op jit(solution)/shard_map/slice | solution.py:286
  1.0 4.9 %collective-permute-start = (bf16[8,10240]{1,0:T(8,128)(2,1)S(1)}, bf16[8,10240]{1,0:T(8,128)(2,1)S(1)}, u32[]{:S(2)}, u32[]{:S(2)}) collective-permute-start(bf16[8,10240]{1,0:T(8,128)(2,1)S(1)} %slice.6), channel_id=1, source_target_pairs={{0,1},{1,2},{2,3},{3,4},{4,5},{5,6},{6,7},{7,8},{8,9},{9,10},{10,1... | collective-permute-start | bytes 491528 | tf_op jit(solution)/shard_map/ppermute | solution.py:23
  5.8 0.0 copy-done
  5.9 0.2 fusion.2
  6.1 0.9 copy.10
  7.0 0.8 broadcast_in_dim.27
  7.7 0.1 broadcast_in_dim.28
  7.9 0.1 broadcast_in_dim.29.skip_ref
  8.0 0.1 copy.12.run_ref
  8.1 0.2 fusion
  8.3 0.1 exp.8
  8.4 0.1 broadcast_in_dim.25
  8.6 0.1 broadcast_in_dim.26.gain_ref
  8.7 0.2 copy.9
  8.9 0.2 copy.11
  9.1 0.2 collective-permute-done.rx.rb.rc
  9.3 0.0 copy-done.3
  9.3 0.0 copy-done.2
  9.3 8.1 %conv_state.1 = (bf16[128,8192]{1,0:T(8,128)(2,1)S(1)}, bf16[128,1024]{1,0:T(8,128)(2,1)S(1)}, bf16[128,1024]{1,0:T(8,128)(2,1)S(1)}, bf16[2,8,4,128,128]{4,3,2,1,0:T(8,128)(2,1)S(1)}) custom-call(bf16[128,10240]{1,0:T(8,128)(2,1)} %pc.1, bf16[128,10240]{1,0:T(8,128)(2,1)} %pc.1, bf16[128,10240]{1,0:T(8,128)(2,1)} %pc.1, ...), custom_call_target="tpu_custom_call" | custom-call | tf_op jit(solution)/shard_map/conv_state/pallas_call | solution.py:309
  17.4 0.0 copy-start.1
  17.4 1.3 %copy-done.1 = bf16[128,8192]{1,0:T(8,128)(2,1)} copy-done((bf16[128,8192]{1,0:T(8,128)(2,1)}, bf16[128,8192]{1,0:T(8,128)(2,1)S(1)}, u32[]{:S(2)}) %copy-start.1) | copy-done | bytes 2097176
  18.7 72.7 %state_scan.1 = bf16[128,8192]{1,0:T(8,128)(2,1)S(1)} custom-call(bf16[2,8,4,128,128]{4,3,2,1,0:T(8,128)(2,1)S(1)} %get-tuple-element.9.state_ref, f32[2,4,8,1,128]{4,3,2,1,0:T(1,128)S(1)} %broadcast_in_dim.26.gain_ref, bf16[128,8192]{1,0:T(8,128)(2,1)} %copy-done.1, bf16[128,1024]{1,0:T(8,128)(2,1)S(1)} %get-tuple-element.11.b_ref, ...), custom_call_target="tpu_custom_call" | custom-call | tf_op jit(solution)/shard_map/state_scan/pallas_call | solution.py:334
  91.5 1.3 %copy.14 = bf16[128,8192]{1,0:T(8,128)(2,1)} copy(bf16[128,8192]{1,0:T(8,128)(2,1)S(1)} %state_scan.1) | data formatting | bytes 4194304
  (1 shorter events, 0.0 us)
Async XLA Ops:
  0.0 5.8 %copy-start = (bf16[128,128]{1,0:T(8,128)(2,1)S(1)}, bf16[128,128]{1,0:T(8,128)(2,1)}, u32[]{:S(2)}) copy-start(bf16[128,128]{1,0:T(8,128)(2,1)} %param.10) | copy-start | bytes 98308
  0.0 9.3 %copy-start.3 = (f32[10240]{0:T(1024)S(1)}, f32[10240]{0:T(1024)}, u32[]{:S(2)}) copy-start(f32[10240]{0:T(1024)} %param.8) | copy-start | bytes 122884
  0.0 9.3 %copy-start.2 = (f32[4,10240]{1,0:T(4,128)S(1)}, f32[4,10240]{1,0:T(4,128)}, u32[]{:S(2)}) copy-start(f32[4,10240]{1,0:T(4,128)} %wc.1) | copy-start | bytes 491524
  1.0 8.3 %collective-permute-start = (bf16[8,10240]{1,0:T(8,128)(2,1)S(1)}, bf16[8,10240]{1,0:T(8,128)(2,1)S(1)}, u32[]{:S(2)}, u32[]{:S(2)}) collective-permute-start(bf16[8,10240]{1,0:T(8,128)(2,1)S(1)} %slice.6), channel_id=1, source_target_pairs={{0,1},{1,2},{2,3},{3,4},{4,5},{5,6},{6,7},{7,8},{8,9},{9,10},{10,1... | collective-permute-start | bytes 491528 | tf_op jit(solution)/shard_map/ppermute | solution.py:23
  17.4 1.3 %copy-start.1 = (bf16[128,8192]{1,0:T(8,128)(2,1)}, bf16[128,8192]{1,0:T(8,128)(2,1)S(1)}, u32[]{:S(2)}) copy-start(bf16[128,8192]{1,0:T(8,128)(2,1)S(1)} %get-tuple-element.10.x_ref) | copy-start | bytes 6291460
